TPU v7x, 512 devices: a whole 4x8x8 slice. The times are simulated.
512 devices in a mesh: dp: 4 (over x), tm: 16 (over y, core), head: 8 (over z).
Axes of the slice: x: 4, y: 8, z: 8, core: 2. Of those that a mesh axis runs over, the one named last changes fastest.
Arguments:
- queries: bfloat16 [512, 32, 3072], P(('dp', 'tm'), None, 'head'), parts along dimension 0, may hold values from -16 to 16
- keys: bfloat16 [512, 32, 3072], P(('dp', 'tm'), None, 'head'), parts along dimension 0, may hold values from -16 to 16
- values: bfloat16 [512, 32, 3072], P(('dp', 'tm'), None, 'head'), parts along dimension 0, may hold values from -6 to 6
- out_grad: bfloat16 [512, 32, 3072], P(('dp', 'tm'), None, 'head'), parts along dimension 0, may hold values from -6 to 6
- out_weight: bfloat16 [3072, 3072], P('tm', 'head'), may hold values from -0.109375 to 0.109375
- lists: int32 [128, 8], P(('dp', 'tm')), parts along dimension 0, may hold values from 0 to 127, as said below
Outputs:
- query_grad: bfloat16 [512, 32, 3072], P(('dp', 'tm'), None, 'head'), parts along dimension 0
- key_grad: bfloat16 [512, 32, 3072], P(('dp', 'tm'), None, 'head'), parts along dimension 0
- value_grad: bfloat16 [512, 32, 3072], P(('dp', 'tm'), None, 'head'), parts along dimension 0
- weight_grad: float32 [12288, 3072], P(('dp', 'tm'), 'head'), parts along dimension 0
There are 4 independent parts, one for each index of `dp`. A program takes and returns all parts, laid end to end along the dimension named above; an argument that names none is the same for every part. Nothing has to cross between parts.
Inputs may be any that keep to these rules, and one draw needn't show every extreme that they name: `lists`: each group names 8 different frames of its rollout. Among the 16 list entries of one time shard's groups, at most 2 name frames owned by any one time shard, and those name at most 1 distinct frame; in every draw, every time shard has some owner for which both bounds are reached.
All inputs are finite; a program needn't handle non-finite values.
Results may differ from a plain program's by a relative error of at most 0.039.
Values may be sent and summed in bfloat16 or wider, within the bound.
No kernel may reach another device: no remote copies, remote signals or barrier semaphores. Data moves between devices by JAX's collectives and lax.ppermute only.
A program may use at most 64 MiB of HBM per device.

v0:
```python
import jax
import jax.numpy as jnp
from jax import lax
from jax.sharding import PartitionSpec as P

HD = 128
CF = 4
RET = 8


def slot_tables(owners, local_frame, slot_index, occupied, myself, capacity):
    slot_range = jnp.arange(capacity, dtype=jnp.int32)
    matches = (
        occupied[:, None, :]
        & (owners[:, None, :] == myself)
        & (slot_index[:, None, :] == slot_range[None, :, None])
    )
    source = jnp.sum(jnp.where(matches, local_frame[:, None, :], 0), axis=2)
    filled = jnp.any(matches, axis=2)
    return (source.reshape(-1), filled.reshape(-1))


def pack_slots(frame_rows, source, filled):
    picked = jnp.take(frame_rows, source, axis=0)
    return jnp.where(filled[:, None, None], picked, jnp.zeros_like(picked))


def per_device(queries, keys, values, out_grad, out_weight, lists):
    frames_dev, frame_tokens, width = queries.shape
    heads_dev = width // HD
    tm_count = lax.axis_size("tm")
    myself = lax.axis_index("tm")
    groups_dev = frames_dev // CF
    entry_count = groups_dev * RET
    token_rows = frames_dev * frame_tokens
    group_rows = CF * frame_tokens
    score_factor = HD ** (-0.5)
    per_owner = max(1, RET // tm_count)
    every_list = lax.all_gather(lists, "tm", axis=0, tiled=True)
    wanted = every_list.reshape(tm_count, entry_count)
    owners = wanted // frames_dev
    local_frame = wanted - owners * frames_dev
    position = jnp.arange(entry_count, dtype=jnp.int32)
    before = (position[:, None] < position[None, :])[None]
    same_owner = owners[:, :, None] == owners[:, None, :]
    same_frame = wanted[:, :, None] == wanted[:, None, :]
    first_seen = jnp.logical_not(jnp.any(same_frame & before, axis=1))
    entry_slot = jnp.sum(same_owner & before, axis=1)
    frame_first = jnp.sum(same_owner & before & first_seen[:, :, None], axis=1)
    frame_slot = jnp.sum(
        jnp.where(same_frame & first_seen[:, :, None], frame_first[:, :, None], 0), axis=1
    )
    my_owner = lax.dynamic_index_in_dim(owners, myself, 0, keepdims=False)
    my_entry_slot = lax.dynamic_index_in_dim(entry_slot, myself, 0, keepdims=False)
    my_frame_slot = lax.dynamic_index_in_dim(frame_slot, myself, 0, keepdims=False)
    frame_source, frame_filled = slot_tables(
        owners, local_frame, frame_slot, first_seen, myself, per_owner
    )
    capacity = groups_dev * per_owner
    source, filled = slot_tables(
        owners, local_frame, entry_slot, jnp.ones_like(first_seen), myself, capacity
    )
    got_keys, got_values = (
        lax.all_to_all(
            pack_slots(keys, source, filled), "tm", split_axis=0, concat_axis=0, tiled=True
        ),
        lax.all_to_all(
            pack_slots(values, source, filled), "tm", split_axis=0, concat_axis=0, tiled=True
        ),
    )
    lookup = my_owner * capacity + my_entry_slot
    grad_full = lax.all_gather(out_grad, "head", axis=2, tiled=True)
    grad_rows = grad_full.reshape(token_rows, grad_full.shape[2])
    columns = grad_rows
    attn_grad = jnp.dot(
        columns,
        lax.all_gather(out_weight, "tm", axis=0, tiled=True),
        preferred_element_type=jnp.float32,
    ).astype(jnp.bfloat16)
    far_keys = jnp.take(got_keys, lookup, axis=0)
    far_values = jnp.take(got_values, lookup, axis=0)
    far_span = RET * frame_tokens
    query_blocks = queries.reshape(groups_dev, group_rows, heads_dev, HD)
    key_set = jnp.concatenate(
        [
            keys.reshape(groups_dev, group_rows, heads_dev, HD),
            far_keys.reshape(groups_dev, far_span, heads_dev, HD),
        ],
        axis=1,
    )
    value_set = jnp.concatenate(
        [
            values.reshape(groups_dev, group_rows, heads_dev, HD),
            far_values.reshape(groups_dev, far_span, heads_dev, HD),
        ],
        axis=1,
    )
    scores = (
        jnp.einsum("cqhd,ckhd->chqk", query_blocks, key_set, preferred_element_type=jnp.float32)
        * score_factor
    )
    row_top = jnp.max(scores, axis=3, keepdims=True)
    weighted = jnp.exp(scores - row_top)
    prob = weighted / jnp.sum(weighted, axis=3, keepdims=True)
    prob_low = prob.astype(jnp.bfloat16)
    attn_out = jnp.einsum(
        "chqk,ckhd->cqhd", prob_low, value_set, preferred_element_type=jnp.float32
    ).astype(jnp.bfloat16)
    grad_blocks = attn_grad.reshape(groups_dev, group_rows, heads_dev, HD)
    row_dot = jnp.sum(grad_blocks.astype(jnp.float32) * attn_out.astype(jnp.float32), axis=3)
    row_dot = jnp.transpose(row_dot, (0, 2, 1))[..., None]
    prob_grad = jnp.einsum(
        "cqhd,ckhd->chqk", grad_blocks, value_set, preferred_element_type=jnp.float32
    )
    score_grad = (prob * (prob_grad - row_dot)).astype(jnp.bfloat16)
    query_grad = (
        jnp.einsum("chqk,ckhd->cqhd", score_grad, key_set, preferred_element_type=jnp.float32)
        * score_factor
    ).astype(jnp.bfloat16)
    key_term = (
        jnp.einsum("chqk,cqhd->ckhd", score_grad, query_blocks, preferred_element_type=jnp.float32)
        * score_factor
    )
    value_term = jnp.einsum(
        "chqk,cqhd->ckhd", prob_low, grad_blocks, preferred_element_type=jnp.float32
    )
    own_dk = key_term[:, :group_rows].reshape(frames_dev, frame_tokens, width)
    own_dv = value_term[:, :group_rows].reshape(frames_dev, frame_tokens, width)
    far_dk = key_term[:, group_rows:].reshape(entry_count, frame_tokens, width)
    far_dv = value_term[:, group_rows:].reshape(entry_count, frame_tokens, width)
    back_slot = my_owner * per_owner + my_frame_slot
    empty = jnp.zeros((tm_count * per_owner, frame_tokens, width), jnp.float32)
    back_keys = empty.at[back_slot].add(far_dk).astype(jnp.bfloat16)
    back_values = empty.at[back_slot].add(far_dv).astype(jnp.bfloat16)
    came_keys, came_values = (
        lax.all_to_all(back_keys, "tm", split_axis=0, concat_axis=0, tiled=True),
        lax.all_to_all(back_values, "tm", split_axis=0, concat_axis=0, tiled=True),
    )
    selector = (
        (frame_source[None, :] == jnp.arange(frames_dev, dtype=jnp.int32)[:, None])
        & frame_filled[None, :]
    ).astype(jnp.bfloat16)
    into_keys = jnp.dot(
        selector, came_keys.reshape(tm_count * per_owner, -1), preferred_element_type=jnp.float32
    )
    into_values = jnp.dot(
        selector, came_values.reshape(tm_count * per_owner, -1), preferred_element_type=jnp.float32
    )
    key_grad = (own_dk + into_keys.reshape(frames_dev, frame_tokens, width)).astype(jnp.bfloat16)
    value_grad = (own_dv + into_values.reshape(frames_dev, frame_tokens, width)).astype(
        jnp.bfloat16
    )
    attn_rows = attn_out.reshape(token_rows, width)
    columns = grad_rows
    weight_grad = lax.psum_scatter(
        lax.dot_general(
            columns, attn_rows, (((0,), (0,)), ((), ())), preferred_element_type=jnp.float32
        ).astype(jnp.bfloat16),
        "tm",
        scatter_dimension=0,
        tiled=True,
    ).astype(jnp.float32)
    return (query_grad.reshape(frames_dev, frame_tokens, width), key_grad, value_grad, weight_grad)


def solution(mesh):
    return jax.shard_map(
        per_device,
        mesh=mesh,
        in_specs=(
            P(("dp", "tm"), None, "head"),
            P(("dp", "tm"), None, "head"),
            P(("dp", "tm"), None, "head"),
            P(("dp", "tm"), None, "head"),
            P("tm", "head"),
            P(("dp", "tm"), None),
        ),
        out_specs=(
            P(("dp", "tm"), None, "head"),
            P(("dp", "tm"), None, "head"),
            P(("dp", "tm"), None, "head"),
            P(("dp", "tm"), "head"),
        ),
        check_vma=False,
    )
```

profile of v0, /device:TPU:1, one launch (start us, length us, event | category | flops | bytes accessed | tf_op | source)
XLA Modules:
  0.0 192.7 jit_solution(17666283749906212261)
XLA Ops:
  8.7 21.2 %all-gather = s32[16,2,8]{2,1,0:T(2,128)S(1)} all-gather(s32[1,2,8]{2,1,0:T(2,128)} %bitcast.101), channel_id=1, replica_groups=mesh['dp'=4,'tm'=16,'head'=8] {'tm'}, dimensions={0}, use_global_device_ids=true | all-gather | bytes 1088 | tf_op jit(solution)/shard_map/all_gather | solution.py:39
  31.0 1.6 gather_fusion.2
  33.4 1.2 select_select_fusion
  34.6 26.1 %all_to_all.20 = bf16[32,32,384]{2,1,0:T(8,128)(2,1)S(1)} all-to-all(bf16[32,32,384]{2,1,0:T(8,128)(2,1)S(1)} %get-tuple-element.34), channel_id=1, replica_groups=mesh['dp'=4,'tm'=16,'head'=8] {'tm'}, dimensions={0} | all-to-all | bytes 1572864 | tf_op jit(solution)/shard_map/all_to_all | solution.py:67
  60.7 3.6 %all-to-all-start = ((bf16[32,32,384]{2,1,0:T(8,128)(2,1)}), bf16[32,32,384]{2,1,0:T(8,128)(2,1)S(1)}, u32[]{:S(2)}, u32[]{:S(2)}) async-start(bf16[32,32,384]{2,1,0:T(8,128)(2,1)} %get-tuple-element.35), calls=%async_computation | async-start | bytes 1572864 | tf_op jit(solution)/shard_map/all_to_all | solution.py:64
  66.0 23.4 %all-to-all-done = bf16[32,32,384]{2,1,0:T(8,128)(2,1)S(1)} async-done(((bf16[32,32,384]{2,1,0:T(8,128)(2,1)}), bf16[32,32,384]{2,1,0:T(8,128)(2,1)S(1)}, u32[]{:S(2)}, u32[]{:S(2)}) %all-to-all-start) | async-done | bytes 786464 | tf_op jit(solution)/shard_map/all_to_all | solution.py:64
  91.6 1.5 fusion.59
  93.1 14.4 %all-gather.6.cloned.1.call-done = bf16[3072,384]{1,0:T(8,128)(2,1)} async-done(((bf16[192,384]{1,0:T(8,128)(2,1)}), bf16[3072,384]{1,0:T(8,128)(2,1)}) %all-gather.6.cloned.1.call-update) | async-done | bytes 2359312 | tf_op jit(solution)/shard_map/all_gather | solution.py:77
  107.6 3.1 %convolution_convert_fusion.1 = bf16[256,384]{1,0:T(8,128)(2,1)S(1)} fusion(bf16[256,3072]{1,0:T(8,128)(2,1)} %bitcast.93, bf16[3072,384]{1,0:T(8,128)(2,1)} %all-gather.6.cloned.1.call-done), kind=kOutput, calls=%fused_computation.22 | convolution fusion | flops 604078080 | bytes 4128768 | tf_op jit(solution)/shard_map/dot_general | solution.py:75
  112.1 2.2 %fusion.1 = bf16[3072,384]{0,1:T(8,128)(2,1)S(1)} fusion(bf16[256,3072]{1,0:T(8,128)(2,1)} %bitcast.94, bf16[48,8,2,128]{3,2,1,0:T(2,128)(2,1)S(1)} %bitcast.97), kind=kOutput, calls=%fused_computation.8 | convolution fusion | flops 605159424 | bytes 4128768 | tf_op jit(solution)/shard_map/dot_general | solution.py:156
  114.3 2.4 %copy.183 = bf16[3072,384]{1,0:T(8,128)(2,1)} copy(bf16[3072,384]{0,1:T(8,128)(2,1)S(1)} %fusion.1) | data formatting | bytes 4718592
  120.0 1.3 reshape.287
  121.3 1.1 copy-done.4
  122.4 1.6 scatter_fusion
  124.8 4.1 %all-to-all-start.2 = ((bf16[16,32,384]{2,1,0:T(8,128)(2,1)}), bf16[16,32,384]{2,1,0:T(8,128)(2,1)S(1)}, u32[]{:S(2)}, u32[]{:S(2)}) async-start(bf16[16,32,384]{2,1,0:T(8,128)(2,1)} %convert_element_type.66), calls=%async_computation.2 | async-start | bytes 786432 | tf_op jit(solution)/shard_map/all_to_all | solution.py:136
  129.1 2.9 %convolution_bitcast_fusion = f32[2,384,3,128]{1,3,2,0:T(8,128)} fusion(bf16[2,128,3,128]{1,3,2,0:T(8,128)(2,1)S(1)} %copy-done.12, f32[2,3,128]{2,1,0:T(4,128)S(1)} %get-tuple-element.38, bf16[2,384,3,128]{3,1,2,0:T(8,128)(2,1)} %copy-done.7, bf16[2,128,3,128]{3,2,1,0:T(4,128)(2,1)S(1)} %copy-done.9), kind=kOutput, calls=%fused_computation.17 | convolution fusion | flops 152175744 | bytes 2165760 | tf_op jit(solution)/shard_map/chqk,cqhd->ckhd/dot_general | solution.py:124
  131.9 1.2 slice.27
  133.5 1.3 reshape.295
  135.9 1.6 scatter_fusion.1
  138.4 6.9 %all-to-all-done.2 = bf16[16,32,384]{2,1,0:T(8,128)(2,1)S(1)} async-done(((bf16[16,32,384]{2,1,0:T(8,128)(2,1)}), bf16[16,32,384]{2,1,0:T(8,128)(2,1)S(1)}, u32[]{:S(2)}, u32[]{:S(2)}) %all-to-all-start.2) | async-done | bytes 393248 | tf_op jit(solution)/shard_map/all_to_all | solution.py:136
  145.2 3.5 %all-to-all-start.3 = ((bf16[16,32,384]{2,1,0:T(8,128)(2,1)}), bf16[16,32,384]{2,1,0:T(8,128)(2,1)S(1)}, u32[]{:S(2)}, u32[]{:S(2)}) async-start(bf16[16,32,384]{2,1,0:T(8,128)(2,1)} %convert_element_type.68), calls=%async_computation.3 | async-start | bytes 786432 | tf_op jit(solution)/shard_map/all_to_all | solution.py:137
  149.4 1.5 fusion.12
  154.0 10.3 %all-to-all-done.3 = bf16[16,32,384]{2,1,0:T(8,128)(2,1)S(1)} async-done(((bf16[16,32,384]{2,1,0:T(8,128)(2,1)}), bf16[16,32,384]{2,1,0:T(8,128)(2,1)S(1)}, u32[]{:S(2)}, u32[]{:S(2)}) %all-to-all-start.3) | async-done | bytes 393248 | tf_op jit(solution)/shard_map/all_to_all | solution.py:137
  165.3 19.0 %reduce-scatter.4.cloned.1.call-done = bf16[192,384]{1,0:T(8,128)(2,1)} async-done(((bf16[3072,384]{1,0:T(8,128)(2,1)}), bf16[192,384]{1,0:T(8,128)(2,1)}) %reduce-scatter.4.cloned.1.call-update) | async-done | bytes 147472
  (111 shorter events, 21.4 us)
Async XLA Ops:
  7.2 25.4 %copy-start.1 = (bf16[8,32,384]{2,1,0:T(8,128)(2,1)S(1)}, bf16[8,32,384]{2,1,0:T(8,128)(2,1)}, u32[]{:S(2)}) copy-start(bf16[8,32,384]{2,1,0:T(8,128)(2,1)} %param.11) | copy-start | bytes 589828
  7.2 85.9 %all-gather.4.cloned.1.call-start = ((), (), s32[]{:S(2)}) async-start(), calls=%async_computation.5 | async-start | bytes 1769472 | tf_op jit(solution)/shard_map/all_gather | solution.py:72
  7.9 99.6 %all-gather.6.cloned.1.call-start = ((), (), s32[]{:S(2)}) async-start(), calls=%async_computation.6 | async-start | bytes 2506752 | tf_op jit(solution)/shard_map/all_gather | solution.py:77
  60.7 3.7 %copy-start = (bf16[8,32,384]{2,1,0:T(8,128)(2,1)S(1)}, bf16[8,32,384]{2,1,0:T(8,128)(2,1)}, u32[]{:S(2)}) copy-start(bf16[8,32,384]{2,1,0:T(8,128)(2,1)} %param.12) | copy-start | bytes 589828
  60.7 3.8 %copy-start.10 = (bf16[8,32,384]{2,1,0:T(8,128)(2,1)S(1)}, bf16[8,32,384]{2,1,0:T(8,128)(2,1)}, u32[]{:S(2)}) copy-start(bf16[8,32,384]{2,1,0:T(8,128)(2,1)} %param.10) | copy-start | bytes 589828
  60.7 28.8 %all-to-all-start = ((bf16[32,32,384]{2,1,0:T(8,128)(2,1)}), bf16[32,32,384]{2,1,0:T(8,128)(2,1)S(1)}, u32[]{:S(2)}, u32[]{:S(2)}) async-start(bf16[32,32,384]{2,1,0:T(8,128)(2,1)} %get-tuple-element.35), calls=%async_computation | async-start | bytes 1572864 | tf_op jit(solution)/shard_map/all_to_all | solution.py:64
  64.3 120.0 %reduce-scatter.4.cloned.1.call-start = ((), (), s32[]{:S(2)}) async-start(), calls=%async_computation.7 | async-start | bytes 2506752
  64.6 53.9 %copy-start.8 = (bf16[2,128,3,128]{3,2,1,0:T(4,128)(2,1)}, bf16[2,128,3,128]{3,2,1,0:T(4,128)(2,1)S(1)}, u32[]{:S(2)}) copy-start(bf16[2,128,3,128]{3,2,1,0:T(4,128)(2,1)S(1)} %reshape.238) | copy-start | bytes 589828
  90.2 1.1 copy-start.13
  91.6 19.4 %copy-start.7 = (bf16[2,384,3,128]{3,1,2,0:T(8,128)(2,1)}, bf16[2,384,3,128]{3,1,2,0:T(8,128)(2,1)S(1)}, u32[]{:S(2)}) copy-start(bf16[2,384,3,128]{3,1,2,0:T(8,128)(2,1)S(1)} %get-tuple-element.43) | copy-start | bytes 1769476
  91.6 19.4 %copy-start.14 = (bf16[2,384,3,128]{3,1,2,0:T(8,128)(2,1)}, bf16[2,384,3,128]{3,1,2,0:T(8,128)(2,1)S(1)}, u32[]{:S(2)}) copy-start(bf16[2,384,3,128]{3,1,2,0:T(8,128)(2,1)S(1)} %get-tuple-element.42) | copy-start | bytes 1769476
  110.9 6.0 %copy-start.11 = (bf16[2,128,3,128]{1,3,2,0:T(8,128)(2,1)}, bf16[2,128,3,128]{1,3,2,0:T(8,128)(2,1)S(1)}, u32[]{:S(2)}) copy-start(bf16[2,128,3,128]{1,3,2,0:T(8,128)(2,1)S(1)} %copy.153) | copy-start | bytes 589828
  116.7 1.1 copy-start.15
  116.7 1.5 copy-start.16
  119.3 30.0 %copy-start.2 = (f32[2,384,3,128]{3,1,2,0:T(8,128)}, f32[2,384,3,128]{3,1,2,0:T(8,128)S(1)}, u32[]{:S(2)}) copy-start(f32[2,384,3,128]{3,1,2,0:T(8,128)S(1)} %fusion.4) | copy-start | bytes 3538948
  121.3 1.1 copy-start.4
  124.0 5.1 %copy-start.9 = (bf16[2,128,3,128]{3,2,1,0:T(4,128)(2,1)S(1)}, bf16[2,128,3,128]{3,2,1,0:T(4,128)(2,1)}, u32[]{:S(2)}) copy-start(bf16[2,128,3,128]{3,2,1,0:T(4,128)(2,1)} %copy-done.8) | copy-start | bytes 589828
  124.0 5.1 %copy-start.12 = (bf16[2,128,3,128]{1,3,2,0:T(8,128)(2,1)S(1)}, bf16[2,128,3,128]{1,3,2,0:T(8,128)(2,1)}, u32[]{:S(2)}) copy-start(bf16[2,128,3,128]{1,3,2,0:T(8,128)(2,1)} %copy-done.11) | copy-start | bytes 589828
  124.8 20.4 %all-to-all-start.2 = ((bf16[16,32,384]{2,1,0:T(8,128)(2,1)}), bf16[16,32,384]{2,1,0:T(8,128)(2,1)S(1)}, u32[]{:S(2)}, u32[]{:S(2)}) async-start(bf16[16,32,384]{2,1,0:T(8,128)(2,1)} %convert_element_type.66), calls=%async_computation.2 | async-start | bytes 786432 | tf_op jit(solution)/shard_map/all_to_all | solution.py:136
  134.8 1.1 copy-start.3
  138.4 11.0 %copy-start.6 = (bf16[2,3,128,384]{2,3,1,0:T(8,128)(2,1)S(1)}, bf16[2,3,128,384]{2,3,1,0:T(8,128)(2,1)}, u32[]{:S(2)}) copy-start(bf16[2,3,128,384]{2,3,1,0:T(8,128)(2,1)} %copy-done.5) | copy-start | bytes 1769476
  145.2 19.0 %all-to-all-start.3 = ((bf16[16,32,384]{2,1,0:T(8,128)(2,1)}), bf16[16,32,384]{2,1,0:T(8,128)(2,1)S(1)}, u32[]{:S(2)}, u32[]{:S(2)}) async-start(bf16[16,32,384]{2,1,0:T(8,128)(2,1)} %convert_element_type.68), calls=%async_computation.3 | async-start | bytes 786432 | tf_op jit(solution)/shard_map/all_to_all | solution.py:137
  149.4 2.6 %slice-start = ((f32[2,384,3,128]{3,1,2,0:T(8,128)}), f32[2,128,3,128]{3,1,2,0:T(8,128)S(1)}, s32[]{:S(2)}) async-start(f32[2,384,3,128]{3,1,2,0:T(8,128)} %copy-done.2), calls=%async_computation.8 | async-start | bytes 786432 | tf_op jit(solution)/shard_map/slice | solution.py:127
  151.1 1.4 slice-start.1
  (1 other events, 0.8 us)
Sparse Core Ops, SparseCore 0:
  10.1 44.7 all-gather.3
  57.0 50.4 all-gather.5
  116.9 67.4 reduce-scatter.3
where the time goes:
time: 196 us; the launch traced here: 193 us
  waiting for transfers between devices  75.5 us (39%)
  blocking collectives  47.3 us (24%)
  local copies, waits for them, and re-layouts  23.6 us (12%)
  between operations  14.3 us (7%)
  matrix products  13.4 us (7%)
  starting transfers between devices  11.3 us (6%)
  other arithmetic  7.44 us (4%)
    all_to_all x1, blocking collectives, per_device(): lax.all_to_all(pack_slots(values, source, filled), 'tm', split_axis=0, co...  26.1 us
    all_to_all x1, waiting for transfers between devices, per_device(): lax.all_to_all(pack_slots(keys, source, filled), 'tm', split_axis=0, conc...  23.4 us
    all_gather x1, blocking collectives, per_device(): every_list = lax.all_gather(lists, 'tm', axis=0, tiled=True)  21.2 us
    unnamed x4, waiting for transfers between devices  20.4 us
    all_gather x1, waiting for transfers between devices, per_device(): lax.all_gather(out_weight, 'tm', axis=0, tiled=True)  14.4 us
    unnamed x41, local copies, waits for them, and re-layouts  11.2 us
    all_to_all x1, waiting for transfers between devices, per_device(): lax.all_to_all(back_values, 'tm', split_axis=0, concat_axis=0, tiled=True)  10.3 us
    all_to_all x1, waiting for transfers between devices, per_device(): lax.all_to_all(back_keys, 'tm', split_axis=0, concat_axis=0, tiled=True)  6.86 us
  transfers between devices with their start and end apart: 6, of which 5 were waited for; matrix products, arithmetic and copies ran while one was open for 15% of the time, Pallas kernels for 0%

commit v1 on v0

v1 whole, which is shorter than its diff:
```python
import functools

import jax
import jax.numpy as jnp
from jax import lax
from jax.experimental import pallas as pl
from jax.experimental.pallas import tpu as pltpu
from jax.sharding import PartitionSpec as P

HD = 128
CF = 4
RET = 8
BF = jnp.bfloat16
F32 = jnp.float32
VMEM = pl.BlockSpec(memory_space=pltpu.VMEM)
SMEM = pl.BlockSpec(memory_space=pltpu.SMEM)
PARAMS = pltpu.CompilerParams(vmem_limit_bytes=40 * 1024 * 1024)
NT = (((1,), (1,)), ((), ()))
NN = (((1,), (0,)), ((), ()))
TN = (((0,), (0,)), ((), ()))


def dot(a, b, dims):
    return lax.dot_general(a, b, dims, preferred_element_type=F32)


def pack_body(source, keys, values, out):
    for shard in range(out.shape[0]):
        frame = source[shard]
        out[shard, 0] = keys[frame]
        out[shard, 1] = values[frame]


def fill_sets(lookup, group, keys, values, got, key_set, value_set):
    tokens = keys.shape[1]
    for f in range(CF):
        rows = pl.ds(f * tokens, tokens)
        key_set[rows, :] = keys[group * CF + f]
        value_set[rows, :] = values[group * CF + f]
    for e in range(RET):
        rows = pl.ds((CF + e) * tokens, tokens)
        owner = lookup[group * RET + e]
        key_set[rows, :] = got[owner, 0]
        value_set[rows, :] = got[owner, 1]


def probabilities(query, key_set):
    scores = dot(query, key_set, NT) * (HD**-0.5)
    weighted = jnp.exp(scores - jnp.max(scores, axis=1, keepdims=True))
    return weighted * (1.0 / jnp.sum(weighted, axis=1, keepdims=True))


def forward_body(lookup, queries, keys, values, got, grad, attn, partial, key_set, value_set):
    frames, tokens, width = queries.shape
    group_rows = CF * tokens
    for group in range(frames // CF):
        fill_sets(lookup, group, keys, values, got, key_set, value_set)
        for head in range(width // HD):
            cols = pl.ds(head * HD, HD)
            query = queries[pl.ds(group * CF, CF), :, cols].reshape(group_rows, HD)
            low = probabilities(query, key_set[:, cols]).astype(BF)
            attn[pl.ds(group * group_rows, group_rows), cols] = dot(
                low, value_set[:, cols], NN
            ).astype(BF)
    chunks, _, chunk = grad.shape
    for c in range(chunks):
        partial[pl.ds(c * chunk, chunk), :] = dot(grad[c], attn[...], TN).astype(BF)


def backward_body(
    lookup, queries, keys, values, got, grad, weight, attn,
    query_grad, back, own_dk, own_dv,
    key_set, value_set, attn_grad, far_dk, far_dv,
):
    frames, tokens, width = queries.shape
    group_rows = CF * tokens
    chunks, _, chunk = grad.shape
    total = dot(grad[0], weight[pl.ds(0, chunk), :], NN)
    for c in range(1, chunks):
        total += dot(grad[c], weight[pl.ds(c * chunk, chunk), :], NN)
    attn_grad[...] = total.astype(BF)
    far_dk[...] = jnp.zeros_like(far_dk)
    far_dv[...] = jnp.zeros_like(far_dv)
    for group in range(frames // CF):
        fill_sets(lookup, group, keys, values, got, key_set, value_set)
        rows = pl.ds(group * group_rows, group_rows)
        for head in range(width // HD):
            cols = pl.ds(head * HD, HD)
            query = queries[pl.ds(group * CF, CF), :, cols].reshape(group_rows, HD)
            prob = probabilities(query, key_set[:, cols])
            low = prob.astype(BF)
            out_grad = attn_grad[rows, cols]
            row_dot = jnp.sum(
                out_grad.astype(F32) * attn[rows, cols].astype(F32), axis=1, keepdims=True
            )
            prob_grad = dot(out_grad, value_set[:, cols], NT)
            score_grad = (prob * (prob_grad - row_dot)).astype(BF)
            dq = (dot(score_grad, key_set[:, cols], NN) * (HD**-0.5)).astype(BF)
            query_grad[pl.ds(group * CF, CF), :, cols] = dq.reshape(CF, tokens, HD)
            dk = dot(score_grad, query, TN) * (HD**-0.5)
            dv = dot(low, out_grad, TN)
            own_dk[rows, cols] = dk[:group_rows]
            own_dv[rows, cols] = dv[:group_rows]
            for e in range(RET):
                owner = lookup[group * RET + e]
                at = slice((CF + e) * tokens, (CF + e + 1) * tokens)
                far_dk[owner, :, cols] += dk[at]
                far_dv[owner, :, cols] += dv[at]
    back[:, 0] = far_dk[...].astype(BF)
    back[:, 1] = far_dv[...].astype(BF)


def finish_body(source, came, own_dk, own_dv, key_grad, value_grad, acc_k, acc_v):
    frames, tokens, width = key_grad.shape
    acc_k[...] = own_dk[...].reshape(frames, tokens, width)
    acc_v[...] = own_dv[...].reshape(frames, tokens, width)
    for shard in range(came.shape[0]):
        frame = source[shard]
        acc_k[frame] += came[shard, 0].astype(F32)
        acc_v[frame] += came[shard, 1].astype(F32)
    key_grad[...] = acc_k[...].astype(BF)
    value_grad[...] = acc_v[...].astype(BF)


def per_device(queries, keys, values, out_grad, out_weight, lists):
    frames, tokens, width = queries.shape
    shards = lax.axis_size("tm")
    heads = lax.axis_size("head")
    rows = frames * tokens
    entries = lists.size
    shape = jax.ShapeDtypeStruct
    myself = lax.axis_index("tm")

    wanted = lax.all_gather(lists, "tm", axis=0, tiled=True).reshape(shards, entries)
    source = jnp.max(jnp.where(wanted // frames == myself, wanted % frames, 0), axis=1)
    lookup = lists.reshape(entries) // frames
    grad = lax.all_gather(out_grad.reshape(rows, width), "head", axis=0, tiled=False)
    weight = lax.all_gather(out_weight, "tm", axis=0, tiled=True)

    packed = pl.pallas_call(
        pack_body,
        out_shape=shape((shards, 2, tokens, width), BF),
        in_specs=[SMEM, VMEM, VMEM],
        out_specs=VMEM,
        compiler_params=PARAMS,
        name="pack",
    )(source, keys, values)
    got = lax.all_to_all(packed, "tm", split_axis=0, concat_axis=0, tiled=True)

    sets = [pltpu.VMEM(((CF + RET) * tokens, width), BF)] * 2
    attn, partial = pl.pallas_call(
        forward_body,
        out_shape=(shape((rows, width), BF), shape((heads * width, width), BF)),
        in_specs=[SMEM] + [VMEM] * 5,
        out_specs=(VMEM, VMEM),
        scratch_shapes=sets,
        compiler_params=PARAMS,
        name="forward",
    )(lookup, queries, keys, values, got, grad)
    weight_grad = lax.psum_scatter(partial, "tm", scatter_dimension=0, tiled=True)

    query_grad, back, own_dk, own_dv = pl.pallas_call(
        backward_body,
        out_shape=(
            shape((frames, tokens, width), BF),
            shape((shards, 2, tokens, width), BF),
            shape((rows, width), F32),
            shape((rows, width), F32),
        ),
        in_specs=[SMEM] + [VMEM] * 7,
        out_specs=(VMEM,) * 4,
        scratch_shapes=sets
        + [pltpu.VMEM((rows, width), BF)]
        + [pltpu.VMEM((shards, tokens, width), F32)] * 2,
        compiler_params=PARAMS,
        name="backward",
    )(lookup, queries, keys, values, got, grad, weight, attn)
    came = lax.all_to_all(back, "tm", split_axis=0, concat_axis=0, tiled=True)

    key_grad, value_grad = pl.pallas_call(
        finish_body,
        out_shape=(shape((frames, tokens, width), BF),) * 2,
        in_specs=[SMEM] + [VMEM] * 3,
        out_specs=(VMEM, VMEM),
        scratch_shapes=[pltpu.VMEM((frames, tokens, width), F32)] * 2,
        compiler_params=PARAMS,
        name="finish",
    )(source, came, own_dk, own_dv)
    return query_grad, key_grad, value_grad, weight_grad.astype(F32)


def solution(mesh):
    tokens = P(("dp", "tm"), None, "head")
    return jax.shard_map(
        per_device,
        mesh=mesh,
        in_specs=(tokens, tokens, tokens, tokens, P("tm", "head"), P(("dp", "tm"), None)),
        out_specs=(tokens, tokens, tokens, P(("dp", "tm"), "head")),
        check_vma=False,
    )
```

time: 196 us -> 181 us (0.923)
  local copies, waits for them, and re-layouts: 23.6 us -> 6.52 us
  matrix products: 13.4 us -> 0 us
  waiting for transfers between devices: 75.5 us -> 88.6 us
  Pallas kernels: 0 us -> 11.9 us
  starting transfers between devices: 11.3 us -> 3.7 us
  other arithmetic: 7.44 us -> 1.91 us
  blocking collectives: 47.3 us -> 51.7 us
    reduce_scatter x0 -> x1, waiting for transfers between devices: none -> 28.9 us  [per_device(): lax.psum_scatter(partial, 'tm', scatter_dimension=0, tiled=True)]
    all_gather x2, waiting for transfers between devices: 14.4 us -> 35.7 us  [the longest x1 35.7 us: per_device(): weight = lax.all_gather(out_weight, 'tm', axis=0, tiled=True)]
    unnamed x4 -> x3, waiting for transfers between devices: 20.4 us -> 1.39 us
    all_to_all x3 -> x1, waiting for transfers between devices: 40.6 us -> 22.6 us  [per_device(): got = lax.all_to_all(packed, 'tm', split_axis=0, concat_axis=0, tiled=True)]
    pallas_call x0 -> x4, Pallas kernels: none -> 11.9 us  [the longest x1 5.18 us: per_device(): pl.pallas_call(backward_body, out_shape=(shape((frames, tokens, width), B...]
    dot_general x9 -> x0, matrix products: 11.8 us -> none  [the longest x1 3.12 us: per_device(): jnp.dot(columns, lax.all_gather(out_weight, 'tm', axis=0, tiled=True), pr...]
    all_to_all x3 -> x1, starting transfers between devices: 11.2 us -> 3.59 us  [per_device(): got = lax.all_to_all(packed, 'tm', split_axis=0, concat_axis=0, tiled=True)]
    unnamed x41 -> x20, local copies, waits for them, and re-layouts: 11.2 us -> 6.36 us
  transfers between devices with their start and end apart: 6 -> 4, of which waited for: 5 -> 3; matrix products, arithmetic and copies ran while one was open for 15% -> 0% of each run, Pallas kernels for 0% -> 7%
where the time goes in v1:
time: 181 us; the launch traced here: 178 us
  waiting for transfers between devices  88.6 us (49%)
  blocking collectives  51.7 us (29%)
  between operations  13.8 us (8%)
  Pallas kernels  11.9 us (7%)
  local copies, waits for them, and re-layouts  6.52 us (4%)
  starting transfers between devices  3.7 us (2%)
  other arithmetic  1.91 us (1%)
    all_gather x1, waiting for transfers between devices, per_device(): weight = lax.all_gather(out_weight, 'tm', axis=0, tiled=True)  35.7 us
    all_to_all x1, blocking collectives, per_device(): came = lax.all_to_all(back, 'tm', split_axis=0, concat_axis=0, tiled=True)  30.5 us
    reduce_scatter x1, waiting for transfers between devices, per_device(): lax.psum_scatter(partial, 'tm', scatter_dimension=0, tiled=True)  28.9 us
    all_to_all x1, waiting for transfers between devices, per_device(): got = lax.all_to_all(packed, 'tm', split_axis=0, concat_axis=0, tiled=True)  22.6 us
    all_gather x1, blocking collectives, per_device(): lax.all_gather(lists, 'tm', axis=0, tiled=True).reshape(shards, entries)  21.2 us
    unnamed x20, local copies, waits for them, and re-layouts  6.36 us
    pallas_call x1, Pallas kernels, per_device(): pl.pallas_call(backward_body, out_shape=(shape((frames, tokens, width), B...  5.18 us
    pallas_call x1, Pallas kernels, per_device(): pl.pallas_call(forward_body, out_shape=(shape((rows, width), BF), shape((...  3.71 us
  transfers between devices with their start and end apart: 4, of which 3 were waited for; matrix products, arithmetic and copies ran while one was open for 0% of the time, Pallas kernels for 7%

profile of v1, /device:TPU:1, one launch (start us, length us, event | category | flops | bytes accessed | tf_op | source)
XLA Modules:
  0.0 178.1 jit_solution(5553925709738380690)
XLA Ops:
  7.2 0.0 all-gather.4.cloned.1.call-start
  7.2 0.7 all-gather.4.cloned.1.call-update
  7.9 0.0 all-gather.6.cloned.1.call-start
  8.0 0.7 all-gather.6.cloned.1.call-update
  8.7 21.2 %all-gather = s32[16,2,8]{2,1,0:T(2,128)S(1)} all-gather(s32[1,2,8]{2,1,0:T(2,128)} %bitcast.5), channel_id=1, replica_groups=mesh['dp'=4,'tm'=16,'head'=8] {'tm'}, dimensions={0}, use_global_device_ids=true | all-gather | bytes 1088 | tf_op jit(solution)/shard_map/all_gather | solution.py:134
  29.8 0.1 fusion.2
  30.0 0.1 reduce_max.14
  30.1 0.1 reduce_max.18.source
  30.2 0.9 copy-done.4
  31.1 0.9 copy-done.6
  32.0 1.5 pack.1
  33.6 3.6 %all-to-all-start = ((bf16[16,2,32,384]{3,2,1,0:T(8,128)(2,1)}), bf16[16,2,32,384]{3,2,1,0:T(8,128)(2,1)S(1)}, u32[]{:S(2)}, u32[]{:S(2)}) async-start(bf16[16,2,32,384]{3,2,1,0:T(8,128)(2,1)} %pack.1), calls=%async_computation | async-start | bytes 1572864 | tf_op jit(solution)/shard_map/all_to_all | solution.py:148
  37.2 0.1 reshape.13
  37.3 22.6 %all-to-all-done.got = bf16[16,2,32,384]{3,2,1,0:T(8,128)(2,1)S(1)} async-done(((bf16[16,2,32,384]{3,2,1,0:T(8,128)(2,1)}), bf16[16,2,32,384]{3,2,1,0:T(8,128)(2,1)S(1)}, u32[]{:S(2)}, u32[]{:S(2)}) %all-to-all-start) | async-done | bytes 786464 | tf_op jit(solution)/shard_map/all_to_all | solution.py:148
  59.9 1.4 copy-done
  61.3 3.7 %forward.1 = (bf16[256,384]{1,0:T(8,128)(2,1)S(1)}, bf16[3072,384]{1,0:T(8,128)(2,1)S(1)}) custom-call(s32[16]{0:T(128)S(1)} %and_select_fusion.lookup, bf16[8,32,384]{2,1,0:T(8,128)(2,1)S(1)} %copy-done.8, bf16[8,32,384]{2,1,0:T(8,128)(2,1)S(1)} %copy-done.5, bf16[8,32,384]{2,1,0:T(8,128)(2,1)S(1)} %copy-done.7, ...), custom_call_target="tpu_custom_call" | custom-call | tf_op jit(solution)/shard_map/forward/pallas_call | solution.py:151
  65.0 1.4 copy-done.3
  66.4 35.7 %all-gather.6.cloned.1.call-done.weight = bf16[3072,384]{1,0:T(8,128)(2,1)} async-done(((bf16[192,384]{1,0:T(8,128)(2,1)}), bf16[3072,384]{1,0:T(8,128)(2,1)}) %all-gather.6.cloned.1.call-update) | async-done | bytes 2359312 | tf_op jit(solution)/shard_map/all_gather | solution.py:138
  102.1 1.7 copy-done.2
  103.8 5.2 %backward.1 = (bf16[8,32,384]{2,1,0:T(8,128)(2,1)}, bf16[16,2,32,384]{3,2,1,0:T(8,128)(2,1)S(1)}, f32[256,384]{1,0:T(8,128)S(1)}, f32[256,384]{1,0:T(8,128)S(1)}) custom-call(s32[16]{0:T(128)S(1)} %and_select_fusion.lookup, bf16[8,32,384]{2,1,0:T(8,128)(2,1)S(1)} %copy-done.8, bf16[8,32,384]{2,1,0:T(8,128)(2,1)S(1)} %copy-done.5, ...), custom_call_target="tpu_custom_call" | custom-call | tf_op jit(solution)/shard_map/backward/pallas_call | solution.py:162
  109.0 30.5 %all_to_all.10.came = bf16[16,2,32,384]{3,2,1,0:T(8,128)(2,1)S(1)} all-to-all(bf16[16,2,32,384]{3,2,1,0:T(8,128)(2,1)S(1)} %get-tuple-element.14), channel_id=1, replica_groups=mesh['dp'=4,'tm'=16,'head'=8] {'tm'}, dimensions={0} | all-to-all | bytes 1572864 | tf_op jit(solution)/shard_map/all_to_all | solution.py:178
  139.5 1.5 finish.1
  141.0 28.9 %reduce-scatter.2.cloned.1.call-done = bf16[192,384]{1,0:T(8,128)(2,1)} async-done(((bf16[3072,384]{1,0:T(8,128)(2,1)}), bf16[192,384]{1,0:T(8,128)(2,1)}) %reduce-scatter.2.cloned.1.call-update) | async-done | bytes 147472 | tf_op jit(solution)/shard_map/reduce_scatter | solution.py:160
  169.9 1.6 convert_element_type.3
  (19 shorter events, 0.1 us)
Async XLA Ops:
  7.2 30.0 %copy-start.9 = (s32[2,8]{1,0:T(2,128)S(1)}, s32[2,8]{1,0:T(2,128)}, u32[]{:S(2)}) copy-start(s32[2,8]{1,0:T(2,128)} %param.11) | copy-start | bytes 196
  7.2 52.7 %copy-start.7 = (bf16[8,32,384]{2,1,0:T(8,128)(2,1)S(1)}, bf16[8,32,384]{2,1,0:T(8,128)(2,1)}, u32[]{:S(2)}) copy-start(bf16[8,32,384]{2,1,0:T(8,128)(2,1)} %values.5) | copy-start | bytes 589828
  7.2 52.7 %copy-start.5 = (bf16[8,32,384]{2,1,0:T(8,128)(2,1)S(1)}, bf16[8,32,384]{2,1,0:T(8,128)(2,1)}, u32[]{:S(2)}) copy-start(bf16[8,32,384]{2,1,0:T(8,128)(2,1)} %keys.5) | copy-start | bytes 589828
  7.2 52.7 %all-gather.4.cloned.1.call-start = ((), (), s32[]{:S(2)}) async-start(), calls=%async_computation.3 | async-start | bytes 1769472 | tf_op jit(solution)/shard_map/all_gather | solution.py:137
  7.9 94.2 %all-gather.6.cloned.1.call-start = ((), (), s32[]{:S(2)}) async-start(), calls=%async_computation.4 | async-start | bytes 2506752 | tf_op jit(solution)/shard_map/all_gather | solution.py:138
  30.2 0.9 copy-start.4
  31.1 0.9 copy-start.6
  32.0 27.8 %copy-start.8 = (bf16[8,32,384]{2,1,0:T(8,128)(2,1)S(1)}, bf16[8,32,384]{2,1,0:T(8,128)(2,1)}, u32[]{:S(2)}) copy-start(bf16[8,32,384]{2,1,0:T(8,128)(2,1)} %queries.3) | copy-start | bytes 589828
  33.6 26.3 %all-to-all-start = ((bf16[16,2,32,384]{3,2,1,0:T(8,128)(2,1)}), bf16[16,2,32,384]{3,2,1,0:T(8,128)(2,1)S(1)}, u32[]{:S(2)}, u32[]{:S(2)}) async-start(bf16[16,2,32,384]{3,2,1,0:T(8,128)(2,1)} %pack.1), calls=%async_computation | async-start | bytes 1572864 | tf_op jit(solution)/shard_map/all_to_all | solution.py:148
  37.1 132.8 %reduce-scatter.2.cloned.1.call-start = ((), (), s32[]{:S(2)}) async-start(), calls=%async_computation.5 | async-start | bytes 2506752 | tf_op jit(solution)/shard_map/reduce_scatter | solution.py:160
  59.9 1.4 copy-start
  61.3 40.9 %copy-start.1 = (bf16[8,256,384]{2,1,0:T(8,128)(2,1)S(1)}, bf16[8,256,384]{2,1,0:T(8,128)(2,1)}, u32[]{:S(2)}) copy-start(bf16[8,256,384]{2,1,0:T(8,128)(2,1)} %all-gather.4.cloned.1.call-done.grad) | copy-start | bytes 4718596
  65.0 1.4 copy-start.3
  102.1 1.7 copy-start.2
Sparse Core Ops, SparseCore 0:
  10.1 45.0 all-gather.3
  57.3 44.7 all-gather.5
  105.0 64.9 reduce-scatter.1

commit v2 on v1

v2 whole, which is shorter than its diff:
```python
import functools

import jax
import jax.numpy as jnp
from jax import lax
from jax.experimental import pallas as pl
from jax.experimental.pallas import tpu as pltpu
from jax.sharding import PartitionSpec as P

HD = 128
CF = 4
RET = 8
LIST_ROWS = 16
BF = jnp.bfloat16
F32 = jnp.float32
HBM = pl.BlockSpec(memory_space=pltpu.HBM)
VMEM = pl.BlockSpec(memory_space=pltpu.VMEM)
SMEM = pl.BlockSpec(memory_space=pltpu.SMEM)
NT = (((1,), (1,)), ((), ()))
NN = (((1,), (0,)), ((), ()))
TN = (((0,), (0,)), ((), ()))


def dot(a, b, dims):
    return lax.dot_general(a, b, dims, preferred_element_type=F32)


def params():
    return pltpu.CompilerParams(vmem_limit_bytes=40 * 1024 * 1024)


def far(array):
    return pltpu.with_memory_space_constraint(array, pltpu.HBM)


def cost(flops, nbytes):
    return pl.CostEstimate(flops=flops, bytes_accessed=nbytes, transcendentals=0)


def pack_body(source, keys, values, out, sems):
    copies = []
    for shard in range(out.shape[0]):
        frame = source[shard]
        for which, held in enumerate((keys, values)):
            copy = pltpu.make_async_copy(
                held.at[frame], out.at[shard, which], sems.at[shard, which]
            )
            copy.start()
            copies.append(copy)
    for copy in copies:
        copy.wait()


def fill_sets(lookup, group, keys, values, got, key_set, value_set):
    tokens = keys.shape[1]
    for f in range(CF):
        rows = pl.ds(f * tokens, tokens)
        key_set[rows, :] = keys[group * CF + f]
        value_set[rows, :] = values[group * CF + f]
    for e in range(RET):
        rows = pl.ds((CF + e) * tokens, tokens)
        owner = lookup[group * RET + e]
        key_set[rows, :] = got[owner, 0]
        value_set[rows, :] = got[owner, 1]


def probabilities(query, key_set):
    scores = dot(query, key_set, NT) * (HD**-0.5)
    weighted = jnp.exp(scores - jnp.max(scores, axis=1, keepdims=True))
    return weighted * (1.0 / jnp.sum(weighted, axis=1, keepdims=True))


def forward_body(
    lookup, core, queries, keys, values, got, grad_far,
    probs, attn, keep, send,
    key_set, value_set, grad, sems,
):
    frames, tokens, width = queries.shape
    heads, group_rows = width // HD, CF * tokens
    chunks = grad.shape[0]
    copies = [
        pltpu.make_async_copy(grad_far.at[c], grad.at[c], sems.at[c]) for c in range(chunks)
    ]
    for copy in copies:
        copy.start()
    for g in range(frames // CF):
        fill_sets(lookup, g, keys, values, got, key_set, value_set)
        for h in range(heads):
            cols = pl.ds(h * HD, HD)
            query = queries[pl.ds(g * CF, CF), :, cols].reshape(group_rows, HD)
            prob = probabilities(query, key_set[:, cols])
            probs[g * heads + h] = prob
            attn[pl.ds(g * group_rows, group_rows), cols] = dot(
                prob.astype(BF), value_set[:, cols], NN
            ).astype(BF)
    first = core[0] == 0
    stripe = keep.shape[1]
    for c, copy in enumerate(copies):
        copy.wait()
        term = dot(grad[c], attn[...], TN).astype(BF)
        top, bottom = term[:stripe], term[stripe:]
        keep[c] = jnp.where(first, top, bottom)
        send[c] = jnp.where(first, bottom, top)


def add_body(ours, theirs, out, total, sems):
    copies = []
    for c in range(out.shape[0]):
        total[c] = (ours[c].astype(F32) + theirs[c].astype(F32)).astype(BF)
        copy = pltpu.make_async_copy(total.at[c], out.at[c], sems.at[c])
        copy.start()
        copies.append(copy)
    for copy in copies:
        copy.wait()


def backward_body(
    parts, lookup, place, queries, keys, values, got, probs, attn, grad_far, quarter, *refs
):
    pieces, refs = refs[: 2 * (parts - 1)], refs[2 * (parts - 1) :]
    query_grad, back, own_dk, own_dv = refs[:4]
    key_set, value_set, attn_grad, grad, weight = refs[4:9]
    far_dk, far_dv, held_dk, held_dv, gsems, wsems, osems = refs[9:]
    frames, tokens, width = queries.shape
    heads, group_rows = width // HD, CF * tokens
    chunks, _, chunk = grad.shape
    shards, _, rows, _ = weight.shape
    dp, core = place[0], place[1]
    half = shards // 2

    copies = [
        pltpu.make_async_copy(grad_far.at[c], grad.at[c], gsems.at[c]) for c in range(chunks)
    ]
    copies.append(
        pltpu.make_async_copy(quarter.at[:, pl.ds(0, rows)], weight.at[:, dp], wsems.at[0])
    )
    for i, piece in enumerate(pieces):
        origin = lax.rem(dp + parts - (1 + i // 2), parts)
        side = core if i % 2 == 0 else 1 - core
        copies.append(
            pltpu.make_async_copy(
                piece, weight.at[pl.ds(side * half, half), origin], wsems.at[1 + i]
            )
        )
    for copy in copies:
        copy.start()
    far_dk[...] = jnp.zeros_like(far_dk)
    far_dv[...] = jnp.zeros_like(far_dv)
    for copy in copies:
        copy.wait()
    per_chunk = chunk // (parts * rows)
    total = None
    for c in range(chunks):
        block = weight[pl.ds(c * per_chunk, per_chunk)].reshape(chunk, width)
        term = dot(grad[c], block, NN)
        total = term if total is None else total + term
    attn_grad[...] = total.astype(BF)

    copies = []
    for g in range(frames // CF):
        fill_sets(lookup, g, keys, values, got, key_set, value_set)
        mine = pl.ds(g * group_rows, group_rows)
        for h in range(heads):
            cols = pl.ds(h * HD, HD)
            query = queries[pl.ds(g * CF, CF), :, cols].reshape(group_rows, HD)
            prob = probs[g * heads + h]
            out_grad = attn_grad[mine, cols]
            row_dot = jnp.sum(
                out_grad.astype(F32) * attn[mine, cols].astype(F32), axis=1, keepdims=True
            )
            prob_grad = dot(out_grad, value_set[:, cols], NT)
            score_grad = (prob * (prob_grad - row_dot)).astype(BF)
            dq = (dot(score_grad, key_set[:, cols], NN) * (HD**-0.5)).astype(BF)
            query_grad[pl.ds(g * CF, CF), :, cols] = dq.reshape(CF, tokens, HD)
            dk = dot(score_grad, query, TN) * (HD**-0.5)
            dv = dot(prob.astype(BF), out_grad, TN)
            held_dk[mine, cols] = dk[:group_rows]
            held_dv[mine, cols] = dv[:group_rows]
            for e in range(RET):
                owner = lookup[g * RET + e]
                at = slice((CF + e) * tokens, (CF + e + 1) * tokens)
                far_dk[owner, :, cols] += dk[at]
                far_dv[owner, :, cols] += dv[at]
        for which, (held, out) in enumerate(((held_dk, own_dk), (held_dv, own_dv))):
            copy = pltpu.make_async_copy(held.at[mine], out.at[mine], osems.at[g, which])
            copy.start()
            copies.append(copy)
    back[:, 0] = far_dk[...].astype(BF)
    back[:, 1] = far_dv[...].astype(BF)
    for copy in copies:
        copy.wait()


def finish_body(source, came, own_dk, own_dv, key_grad, value_grad, acc_k, acc_v):
    frames, tokens, width = key_grad.shape
    acc_k[...] = own_dk[...].reshape(frames, tokens, width)
    acc_v[...] = own_dv[...].reshape(frames, tokens, width)
    for shard in range(came.shape[0]):
        frame = source[shard]
        acc_k[frame] += came[shard, 0].astype(F32)
        acc_v[frame] += came[shard, 1].astype(F32)
    key_grad[...] = acc_k[...].astype(BF)
    value_grad[...] = acc_v[...].astype(BF)


def per_device(queries, keys, values, out_grad, out_weight, lists):
    frames, tokens, width = queries.shape
    parts, chips = lax.axis_size("dp"), lax.axis_size("y")
    shards, heads = 2 * chips, lax.axis_size("head")
    dp, core = lax.axis_index("dp"), lax.axis_index("core")
    time = ("y", "core")
    myself = lax.axis_index(time)
    rows, entries, groups = frames * tokens, lists.size, frames // CF
    stripe = out_weight.shape[0]
    part_rows, half = stripe // parts, shards // 2
    shape = jax.ShapeDtypeStruct
    dma = pltpu.SemaphoreType.DMA
    other = [(0, 1), (1, 0)]

    grad = lax.all_gather(out_grad.reshape(rows, width), "head", axis=0, tiled=False)

    part = lax.dynamic_slice_in_dim(out_weight, dp * part_rows, part_rows, 0)
    names = jnp.zeros((LIST_ROWS, width), BF).at[0, :entries].set(lists.reshape(entries).astype(BF))
    quarter = lax.all_gather(jnp.concatenate([part, names], axis=0), time, axis=0, tiled=False)
    wanted = quarter[:, part_rows, :entries].astype(jnp.int32)
    source = jnp.max(jnp.where(wanted // frames == myself, wanted % frames, 0), axis=1)
    lookup = lists.reshape(entries) // frames

    packed = pl.pallas_call(
        pack_body,
        out_shape=shape((shards, 2, tokens, width), BF),
        in_specs=[SMEM, HBM, HBM],
        out_specs=HBM,
        scratch_shapes=[dma((shards, 2))],
        compiler_params=params(),
        cost_estimate=cost(0, 4 * shards * tokens * width * 2),
        name="pack",
    )(source, keys, values)
    got = lax.all_to_all(packed, time, split_axis=0, concat_axis=0, tiled=True)

    mine = lax.dynamic_slice_in_dim(quarter, core * half, half, 0)[:, :part_rows]
    halves = [
        lax.ppermute(mine, "dp", [(i, (i + s) % parts) for i in range(parts)])
        for s in range(1, parts)
    ]
    got, *halves = lax.optimization_barrier((got, *halves))
    pieces = []
    for piece in halves:
        pieces += [piece, lax.ppermute(piece, "core", other)]

    partial = shape((heads, stripe, width), BF)
    key_rows = (CF + RET) * tokens
    sets = pltpu.VMEM((key_rows, width), BF)
    chunks = pltpu.VMEM((heads, rows, width), BF)
    token_sum = pltpu.VMEM((rows, width), F32)
    far_sum = pltpu.VMEM((shards, tokens, width), F32)
    probs, attn, keep, send = pl.pallas_call(
        forward_body,
        out_shape=(
            shape((groups * width // HD, CF * tokens, key_rows), F32),
            shape((rows, width), BF),
            partial,
            partial,
        ),
        in_specs=[SMEM] * 2 + [VMEM] * 4 + [HBM],
        out_specs=(VMEM,) * 4,
        scratch_shapes=[sets, sets, chunks, dma((heads,))],
        compiler_params=params(),
        cost_estimate=cost(4 * 10**9, 8 * 10**6),
        name="forward",
    )(lookup, core[None], queries, keys, values, got, far(grad))

    theirs = lax.ppermute(send, "core", other)
    chip_sum = pl.pallas_call(
        add_body,
        out_shape=partial,
        in_specs=[VMEM, VMEM],
        out_specs=HBM,
        scratch_shapes=[pltpu.VMEM(partial.shape, BF), dma((heads,))],
        compiler_params=params(),
        cost_estimate=cost(10**6, 4 * 10**6),
        name="add",
    )(keep, theirs)
    weight_grad = lax.psum_scatter(chip_sum, "y", scatter_dimension=0, tiled=False)

    query_grad, back, own_dk, own_dv = pl.pallas_call(
        functools.partial(backward_body, parts),
        out_shape=(
            shape((frames, tokens, width), BF),
            shape((shards, 2, tokens, width), BF),
            shape((rows, width), F32),
            shape((rows, width), F32),
        ),
        in_specs=[SMEM] * 2 + [VMEM] * 6 + [HBM] * (2 + len(pieces)),
        out_specs=(VMEM, VMEM, HBM, HBM),
        scratch_shapes=[
            sets,
            sets,
            pltpu.VMEM((rows, width), BF),
            chunks,
            pltpu.VMEM((shards, parts, part_rows, width), BF),
            far_sum,
            far_sum,
            token_sum,
            token_sum,
            dma((heads,)),
            dma((1 + len(pieces),)),
            dma((groups, 2)),
        ],
        compiler_params=params(),
        cost_estimate=cost(6 * 10**9, 9 * 10**6),
        name="backward",
    )(
        lookup, jnp.stack([dp, core]), queries, keys, values, got, probs, attn,
        far(grad), far(quarter), *[far(p) for p in pieces],
    )
    came = lax.all_to_all(back, time, split_axis=0, concat_axis=0, tiled=True)

    key_grad, value_grad = pl.pallas_call(
        finish_body,
        out_shape=(shape((frames, tokens, width), BF),) * 2,
        in_specs=[SMEM] + [VMEM] * 3,
        out_specs=(VMEM, VMEM),
        scratch_shapes=[pltpu.VMEM((frames, tokens, width), F32)] * 2,
        compiler_params=params(),
        cost_estimate=cost(10**6, 3 * 10**6),
        name="finish",
    )(source, came, own_dk, own_dv)
    return query_grad, key_grad, value_grad, weight_grad.astype(F32)


def solution(mesh):
    dp, time, head = mesh.devices.shape
    fine = jax.sharding.Mesh(
        mesh.devices.reshape(dp, time // 2, 2, head), ("dp", "y", "core", "head")
    )
    tokens = P(("dp", "y", "core"), None, "head")
    return jax.shard_map(
        per_device,
        mesh=fine,
        in_specs=(
            tokens, tokens, tokens, tokens,
            P(("y", "core"), "head"),
            P(("dp", "y", "core"), None),
        ),
        out_specs=(tokens, tokens, tokens, P(("dp", "y", "core"), "head")),
        check_vma=False,
    )
```

time: 181 us -> 134 us (0.74); the launches traced: 178 us -> 133 us
  waiting for transfers between devices: 88.6 us -> 18.5 us
  starting transfers between devices: 3.7 us -> 21.1 us
  blocking collectives: 51.7 us -> 58.2 us
  Pallas kernels: 11.9 us -> 17.6 us
  local copies, waits for them, and re-layouts: 6.52 us -> 0.97 us
    all_gather x1 -> x0, waiting for transfers between devices: 35.7 us -> none  [per_device(): weight = lax.all_gather(out_weight, 'tm', axis=0, tiled=True)]
    reduce_scatter x1, waiting for transfers between devices: 28.9 us -> 0.01 us  [per_device(): lax.psum_scatter(chip_sum, 'y', scatter_dimension=0, tiled=False)]
    all_to_all x1, waiting for transfers between devices: 22.6 us -> 2.57 us  [per_device(): got = lax.all_to_all(packed, time, split_axis=0, concat_axis=0, tiled=True)]
    ppermute x0 -> x7, starting transfers between devices: none -> 17.3 us  [the longest x3 9.02 us: per_device(): lax.ppermute(mine, 'dp', [(i, (i + s) % parts) for i in range(parts)])]
    ppermute x0 -> x7, waiting for transfers between devices: none -> 15.2 us  [the longest x3 10.9 us: per_device(): lax.ppermute(mine, 'dp', [(i, (i + s) % parts) for i in range(parts)])]
    unnamed x20 -> x24, local copies, waits for them, and re-layouts: 6.36 us -> 0.76 us
    pallas_call x2 -> x3, Pallas kernels: 8.89 us -> 14.4 us  [the longest x1 8 us: per_device(): pl.pallas_call(functools.partial(backward_body, parts), out_shape=(shape(...]
    all_to_all x1, blocking collectives: 30.5 us -> 34.6 us  [per_device(): came = lax.all_to_all(back, time, split_axis=0, concat_axis=0, tiled=True)]
  transfers between devices with their start and end apart: 4 -> 10, of which waited for: 3 -> 6; matrix products, arithmetic and copies ran while one was open for 0% -> 1% of each run, Pallas kernels for 7% -> 8%
where the time goes in v2:
time: 134 us; the launch traced here: 133 us
  blocking collectives  58.2 us (43%)
  starting transfers between devices  21.1 us (16%)
  waiting for transfers between devices  18.5 us (14%)
  Pallas kernels  17.6 us (13%)
  between operations  14.3 us (11%)
  other arithmetic  2.56 us (2%)
    all_to_all x1, blocking collectives, per_device(): came = lax.all_to_all(back, time, split_axis=0, concat_axis=0, tiled=True)  34.6 us
    all_gather x1, blocking collectives, per_device(): lax.all_gather(jnp.concatenate([part, names], axis=0), time, axis=0, tile...  23.6 us
    ppermute x3, waiting for transfers between devices, per_device(): lax.ppermute(mine, 'dp', [(i, (i + s) % parts) for i in range(parts)])  10.9 us
    ppermute x3, starting transfers between devices, per_device(): lax.ppermute(mine, 'dp', [(i, (i + s) % parts) for i in range(parts)])  9.02 us
    pallas_call x1, Pallas kernels, per_device(): pl.pallas_call(functools.partial(backward_body, parts), out_shape=(shape(...  8 us
    ppermute x3, starting transfers between devices, per_device(): pieces += [piece, lax.ppermute(piece, 'core', other)]  6.37 us
    pallas_call x1, Pallas kernels, per_device(): pl.pallas_call(forward_body, out_shape=(shape((groups * width // HD, CF *...  5.22 us
    all_to_all x1, starting transfers between devices, per_device(): got = lax.all_to_all(packed, time, split_axis=0, concat_axis=0, tiled=True)  3.71 us
  transfers between devices with their start and end apart: 10, of which 6 were waited for; matrix products, arithmetic and copies ran while one was open for 1% of the time, Pallas kernels for 8%

profile of v2, /device:TPU:1, one launch (start us, length us, event | category | flops | bytes accessed | tf_op | source)
XLA Modules:
  0.0 133.2 jit_solution(2178380453684885657)
XLA Ops:
  7.9 0.7 convert_element_type.23
  8.7 23.6 %all-gather = bf16[1024,384]{1,0:T(8,128)(2,1)S(1)} all-gather(bf16[64,384]{1,0:T(8,128)(2,1)S(1)} %fusion.1), channel_id=2, replica_groups=mesh['dp'=4,'y'=8,'core'=2,'head'=8] {'y','core'}, dimensions={0}, use_global_device_ids=true | all-gather | bytes 835584 | tf_op jit(solution)/shard_map/all_gather | solution.py:224
  32.4 1.7 %pack.1 = bf16[16,2,32,384]{3,2,1,0:T(8,128)(2,1)} custom-call(s32[16]{0:T(128)S(1)} %fusion.4.source, bf16[8,32,384]{2,1,0:T(8,128)(2,1)S(1)} %copy-done.1, bf16[8,32,384]{2,1,0:T(8,128)(2,1)S(1)} %copy-done.2), custom_call_target="tpu_custom_call" | custom-call | bytes 1572864 | tf_op jit(solution)/shard_map/pack/pallas_call | solution.py:229
  34.2 3.7 %all-to-all-start = ((bf16[16,2,32,384]{3,2,1,0:T(8,128)(2,1)}), bf16[16,2,32,384]{3,2,1,0:T(8,128)(2,1)S(1)}, u32[]{:S(2)}, u32[]{:S(2)}) async-start(bf16[16,2,32,384]{3,2,1,0:T(8,128)(2,1)} %pack.1), calls=%async_computation | async-start | bytes 1572864 | tf_op jit(solution)/shard_map/all_to_all | solution.py:239
  38.0 1.9 %collective-permute-start = (bf16[8,48,384]{2,1,0:T(8,128)(2,1)S(1)}, bf16[8,48,384]{2,1,0:T(8,128)(2,1)S(1)}, u32[]{:S(2)}, u32[]{:S(2)}) collective-permute-start(bf16[8,48,384]{2,1,0:T(8,128)(2,1)S(1)} %constant_dynamic-slice_fusion), channel_id=1, source_target_pairs={{0,128},{128,256},{256,384},{384,0},{1,129},{129,257},{257,385},{3... | collective-permute-start | bytes 884744 | tf_op jit(solution)/shard_map/ppermute | solution.py:243
  39.9 4.0 %collective-permute-start.1 = (bf16[8,48,384]{2,1,0:T(8,128)(2,1)S(1)}, bf16[8,48,384]{2,1,0:T(8,128)(2,1)S(1)}, u32[]{:S(2)}, u32[]{:S(2)}) collective-permute-start(bf16[8,48,384]{2,1,0:T(8,128)(2,1)S(1)} %constant_dynamic-slice_fusion), channel_id=1, source_target_pairs={{0,256},{128,384},{256,0},{384,128},{1,257},{129,385},{257,1},{385... | collective-permute-start | bytes 884744 | tf_op jit(solution)/shard_map/ppermute | solution.py:243
  44.0 3.1 %collective-permute-start.2 = (bf16[8,48,384]{2,1,0:T(8,128)(2,1)S(1)}, bf16[8,48,384]{2,1,0:T(8,128)(2,1)S(1)}, u32[]{:S(2)}, u32[]{:S(2)}) collective-permute-start(bf16[8,48,384]{2,1,0:T(8,128)(2,1)S(1)} %constant_dynamic-slice_fusion), channel_id=1, source_target_pairs={{0,384},{128,0},{256,128},{384,256},{1,385},{129,1},{257,129},{385... | collective-permute-start | bytes 884744 | tf_op jit(solution)/shard_map/ppermute | solution.py:243
  47.2 2.7 %collective-permute-done.refs_0_ = bf16[8,48,384]{2,1,0:T(8,128)(2,1)S(1)} collective-permute-done((bf16[8,48,384]{2,1,0:T(8,128)(2,1)S(1)}, bf16[8,48,384]{2,1,0:T(8,128)(2,1)S(1)}, u32[]{:S(2)}, u32[]{:S(2)}) %collective-permute-start) | collective-permute-done | bytes 294944 | tf_op jit(solution)/shard_map/ppermute | solution.py:243
  49.9 5.6 %collective-permute-done.1.refs_2_ = bf16[8,48,384]{2,1,0:T(8,128)(2,1)S(1)} collective-permute-done((bf16[8,48,384]{2,1,0:T(8,128)(2,1)S(1)}, bf16[8,48,384]{2,1,0:T(8,128)(2,1)S(1)}, u32[]{:S(2)}, u32[]{:S(2)}) %collective-permute-start.1) | collective-permute-done | bytes 294944 | tf_op jit(solution)/shard_map/ppermute | solution.py:243
  55.5 2.5 %collective-permute-done.2.refs_4_ = bf16[8,48,384]{2,1,0:T(8,128)(2,1)S(1)} collective-permute-done((bf16[8,48,384]{2,1,0:T(8,128)(2,1)S(1)}, bf16[8,48,384]{2,1,0:T(8,128)(2,1)S(1)}, u32[]{:S(2)}, u32[]{:S(2)}) %collective-permute-start.2) | collective-permute-done | bytes 294944 | tf_op jit(solution)/shard_map/ppermute | solution.py:243
  58.0 2.6 %all-to-all-done.got = bf16[16,2,32,384]{3,2,1,0:T(8,128)(2,1)S(1)} async-done(((bf16[16,2,32,384]{3,2,1,0:T(8,128)(2,1)}), bf16[16,2,32,384]{3,2,1,0:T(8,128)(2,1)S(1)}, u32[]{:S(2)}, u32[]{:S(2)}) %all-to-all-start) | async-done | bytes 786464 | tf_op jit(solution)/shard_map/all_to_all | solution.py:239
  60.6 5.2 %forward.1 = (f32[6,128,384]{2,1,0:T(8,128)S(1)}, bf16[256,384]{1,0:T(8,128)(2,1)S(1)}, bf16[8,192,384]{2,1,0:T(8,128)(2,1)S(1)}, bf16[8,192,384]{2,1,0:T(8,128)(2,1)S(1)}) custom-call(s32[16]{0:T(128)S(1)} %and_select_fusion.lookup, s32[1]{0:T(128)} %bitcast.1.core, bf16[8,32,384]{2,1,0:T(8,128)(2,1)S(1)} %copy-done.3, bf16[8,32,384]{2,1,0:T(8,128)(2,1)S(1)} %copy-done.1, ...), custom_call_target="tpu_custom_call" | custom-call | flops 4000000000 | bytes 8000000 | tf_op jit(solution)/shard_map/forward/pallas_call | solution.py:257
  65.9 1.9 %collective-permute-start.6 = (bf16[8,192,384]{2,1,0:T(8,128)(2,1)S(1)}, bf16[8,192,384]{2,1,0:T(8,128)(2,1)S(1)}, u32[]{:S(2)}, u32[]{:S(2)}) collective-permute-start(bf16[8,192,384]{2,1,0:T(8,128)(2,1)S(1)} %get-tuple-element.43), channel_id=1, source_target_pairs={{0,8},{8,0},{1,9},{9,1},{2,10},{10,2},{3,11},{11,3},{4,12},{12,4},... | collective-permute-start | bytes 3538952 | tf_op jit(solution)/shard_map/ppermute | solution.py:273
  67.8 2.8 %collective-permute-done.6.theirs = bf16[8,192,384]{2,1,0:T(8,128)(2,1)S(1)} collective-permute-done((bf16[8,192,384]{2,1,0:T(8,128)(2,1)S(1)}, bf16[8,192,384]{2,1,0:T(8,128)(2,1)S(1)}, u32[]{:S(2)}, u32[]{:S(2)}) %collective-permute-start.6) | collective-permute-done | bytes 1179680 | tf_op jit(solution)/shard_map/ppermute | solution.py:273
  70.6 1.1 add.36
  71.8 2.0 %collective-permute-start.3 = (bf16[8,48,384]{2,1,0:T(8,128)(2,1)S(1)}, bf16[8,48,384]{2,1,0:T(8,128)(2,1)S(1)}, u32[]{:S(2)}, u32[]{:S(2)}) collective-permute-start(bf16[8,48,384]{2,1,0:T(8,128)(2,1)S(1)} %collective-permute-done.refs_0_), channel_id=1, source_target_pairs={{0,8},{8,0},{1,9},{9,1},{2,10},{10,2},{3,11},{11,3},{4,12},{12,4},... | collective-permute-start | bytes 884744 | tf_op jit(solution)/shard_map/ppermute | solution.py:249
  73.8 2.3 %collective-permute-start.4 = (bf16[8,48,384]{2,1,0:T(8,128)(2,1)S(1)}, bf16[8,48,384]{2,1,0:T(8,128)(2,1)S(1)}, u32[]{:S(2)}, u32[]{:S(2)}) collective-permute-start(bf16[8,48,384]{2,1,0:T(8,128)(2,1)S(1)} %collective-permute-done.1.refs_2_), channel_id=1, source_target_pairs={{0,8},{8,0},{1,9},{9,1},{2,10},{10,2},{3,11},{11,3},{4,12},{12,4},... | collective-permute-start | bytes 884744 | tf_op jit(solution)/shard_map/ppermute | solution.py:249
  76.1 2.0 %collective-permute-start.5 = (bf16[8,48,384]{2,1,0:T(8,128)(2,1)}, bf16[8,48,384]{2,1,0:T(8,128)(2,1)S(1)}, u32[]{:S(2)}, u32[]{:S(2)}) collective-permute-start(bf16[8,48,384]{2,1,0:T(8,128)(2,1)} %copy-done.7), channel_id=1, source_target_pairs={{0,8},{8,0},{1,9},{9,1},{2,10},{10,2},{3,11},{11,3},{4,12},{12,4},... | collective-permute-start | bytes 884744 | tf_op jit(solution)/shard_map/ppermute | solution.py:249
  78.3 1.5 %collective-permute-done.5.refs_5_ = bf16[8,48,384]{2,1,0:T(8,128)(2,1)S(1)} collective-permute-done((bf16[8,48,384]{2,1,0:T(8,128)(2,1)}, bf16[8,48,384]{2,1,0:T(8,128)(2,1)S(1)}, u32[]{:S(2)}, u32[]{:S(2)}) %collective-permute-start.5) | collective-permute-done | bytes 294944 | tf_op jit(solution)/shard_map/ppermute | solution.py:249
  79.8 0.7 copy-done.10
  80.5 8.0 %backward.1 = (bf16[8,32,384]{2,1,0:T(8,128)(2,1)}, bf16[16,2,32,384]{3,2,1,0:T(8,128)(2,1)S(1)}, f32[256,384]{1,0:T(8,128)S(1)}, f32[256,384]{1,0:T(8,128)S(1)}) custom-call(s32[16]{0:T(128)S(1)} %and_select_fusion.lookup, s32[2]{0:T(128)S(1)} %pad_add_fusion.place, bf16[8,32,384]{2,1,0:T(8,128)(2,1)S(1)} %copy-done.3, bf16[8,32,384]{2,1,0:T(8,128)(2,1)S(1)} %copy-done.1, ...), custom_call_target="tpu_custom_call" | custom-call | flops 6000000000 | bytes 9000000 | tf_op jit(solution)/shard_map/backward/pallas_call | solution.py:286
  88.5 34.6 %all_to_all.10.came = bf16[16,2,32,384]{3,2,1,0:T(8,128)(2,1)S(1)} all-to-all(bf16[16,2,32,384]{3,2,1,0:T(8,128)(2,1)S(1)} %get-tuple-element.37), channel_id=1, replica_groups=mesh['dp'=4,'y'=8,'core'=2,'head'=8] {'y','core'}, dimensions={0} | all-to-all | bytes 1572864 | tf_op jit(solution)/shard_map/all_to_all | solution.py:317
  123.2 1.5 %finish.1 = (bf16[8,32,384]{2,1,0:T(8,128)(2,1)}, bf16[8,32,384]{2,1,0:T(8,128)(2,1)}) custom-call(s32[16]{0:T(128)S(1)} %fusion.4.source, bf16[16,2,32,384]{3,2,1,0:T(8,128)(2,1)S(1)} %all_to_all.10.came, f32[256,384]{1,0:T(8,128)S(1)} %get-tuple-element.38.own_dk, f32[256,384]{1,0:T(8,128)S(1)} %get-tuple-element.39.own_dv), custom_call_target="tpu_custom_call" | custom-call | flops 1000000 | bytes 3000000 | tf_op jit(solution)/shard_map/finish/pallas_call | solution.py:319
  124.7 1.6 %bitcast_convert_fusion = f32[192,384]{1,0:T(8,128)} fusion(bf16[1,192,384]{2,1,0:T(8,128)(2,1)} %reduce-scatter.2.cloned.1.call-done), kind=kLoop, calls=%fused_computation | loop fusion | flops 73728 | bytes 442368 | tf_op jit(solution)/shard_map/convert_element_type | solution.py:329
  (40 shorter events, 1.3 us)
Async XLA Ops:
  7.2 1.6 %copy-start = (bf16[192,384]{1,0:T(8,128)(2,1)S(1)}, bf16[192,384]{1,0:T(8,128)(2,1)}, u32[]{:S(2)}) copy-start(bf16[192,384]{1,0:T(8,128)(2,1)} %param.12) | copy-start | bytes 442372
  7.2 25.3 %copy-start.2 = (bf16[8,32,384]{2,1,0:T(8,128)(2,1)S(1)}, bf16[8,32,384]{2,1,0:T(8,128)(2,1)}, u32[]{:S(2)}) copy-start(bf16[8,32,384]{2,1,0:T(8,128)(2,1)} %values.5) | copy-start | bytes 589828
  7.2 25.3 %copy-start.1 = (bf16[8,32,384]{2,1,0:T(8,128)(2,1)S(1)}, bf16[8,32,384]{2,1,0:T(8,128)(2,1)}, u32[]{:S(2)}) copy-start(bf16[8,32,384]{2,1,0:T(8,128)(2,1)} %keys.5) | copy-start | bytes 589828
  7.2 53.4 %all-gather.3.cloned.1.call-start = ((), (), s32[]{:S(2)}) async-start(), calls=%async_computation.3 | async-start | bytes 1769472 | tf_op jit(solution)/shard_map/all_gather | solution.py:220
  32.3 5.7 %copy-start.4 = (bf16[1024,384]{1,0:T(8,128)(2,1)}, bf16[1024,384]{1,0:T(8,128)(2,1)S(1)}, u32[]{:S(2)}) copy-start(bf16[1024,384]{1,0:T(8,128)(2,1)S(1)} %all-gather) | copy-start | bytes 2359300
  34.2 12.9 %copy-start.11 = (s32[2,8]{1,0:T(2,128)S(1)}, s32[2,8]{1,0:T(2,128)}, u32[]{:S(2)}) copy-start(s32[2,8]{1,0:T(2,128)} %param.13) | copy-start | bytes 196
  34.2 26.4 %copy-start.3 = (bf16[8,32,384]{2,1,0:T(8,128)(2,1)S(1)}, bf16[8,32,384]{2,1,0:T(8,128)(2,1)}, u32[]{:S(2)}) copy-start(bf16[8,32,384]{2,1,0:T(8,128)(2,1)} %queries.3) | copy-start | bytes 589828
  34.2 26.4 %all-to-all-start = ((bf16[16,2,32,384]{3,2,1,0:T(8,128)(2,1)}), bf16[16,2,32,384]{3,2,1,0:T(8,128)(2,1)S(1)}, u32[]{:S(2)}, u32[]{:S(2)}) async-start(bf16[16,2,32,384]{3,2,1,0:T(8,128)(2,1)} %pack.1), calls=%async_computation | async-start | bytes 1572864 | tf_op jit(solution)/shard_map/all_to_all | solution.py:239
  37.9 86.8 %reduce-scatter.2.cloned.1.call-start = ((), (), s32[]{:S(2)}) async-start(), calls=%async_computation.4 | async-start | bytes 1327104 | tf_op jit(solution)/shard_map/reduce_scatter | solution.py:284
  38.0 11.9 %collective-permute-start = (bf16[8,48,384]{2,1,0:T(8,128)(2,1)S(1)}, bf16[8,48,384]{2,1,0:T(8,128)(2,1)S(1)}, u32[]{:S(2)}, u32[]{:S(2)}) collective-permute-start(bf16[8,48,384]{2,1,0:T(8,128)(2,1)S(1)} %constant_dynamic-slice_fusion), channel_id=1, source_target_pairs={{0,128},{128,256},{256,384},{384,0},{1,129},{129,257},{257,385},{3... | collective-permute-start | bytes 884744 | tf_op jit(solution)/shard_map/ppermute | solution.py:243
  39.9 15.6 %collective-permute-start.1 = (bf16[8,48,384]{2,1,0:T(8,128)(2,1)S(1)}, bf16[8,48,384]{2,1,0:T(8,128)(2,1)S(1)}, u32[]{:S(2)}, u32[]{:S(2)}) collective-permute-start(bf16[8,48,384]{2,1,0:T(8,128)(2,1)S(1)} %constant_dynamic-slice_fusion), channel_id=1, source_target_pairs={{0,256},{128,384},{256,0},{384,128},{1,257},{129,385},{257,1},{385... | collective-permute-start | bytes 884744 | tf_op jit(solution)/shard_map/ppermute | solution.py:243
  44.0 14.1 %collective-permute-start.2 = (bf16[8,48,384]{2,1,0:T(8,128)(2,1)S(1)}, bf16[8,48,384]{2,1,0:T(8,128)(2,1)S(1)}, u32[]{:S(2)}, u32[]{:S(2)}) collective-permute-start(bf16[8,48,384]{2,1,0:T(8,128)(2,1)S(1)} %constant_dynamic-slice_fusion), channel_id=1, source_target_pairs={{0,384},{128,0},{256,128},{384,256},{1,385},{129,1},{257,129},{385... | collective-permute-start | bytes 884744 | tf_op jit(solution)/shard_map/ppermute | solution.py:243
  49.9 21.9 %copy-start.5 = (bf16[8,48,384]{2,1,0:T(8,128)(2,1)}, bf16[8,48,384]{2,1,0:T(8,128)(2,1)S(1)}, u32[]{:S(2)}) copy-start(bf16[8,48,384]{2,1,0:T(8,128)(2,1)S(1)} %collective-permute-done.refs_0_) | copy-start | bytes 884740
  55.5 18.3 %copy-start.6 = (bf16[8,48,384]{2,1,0:T(8,128)(2,1)}, bf16[8,48,384]{2,1,0:T(8,128)(2,1)S(1)}, u32[]{:S(2)}) copy-start(bf16[8,48,384]{2,1,0:T(8,128)(2,1)S(1)} %collective-permute-done.1.refs_2_) | copy-start | bytes 884740
  58.0 2.6 %copy-start.7 = (bf16[8,48,384]{2,1,0:T(8,128)(2,1)}, bf16[8,48,384]{2,1,0:T(8,128)(2,1)S(1)}, u32[]{:S(2)}) copy-start(bf16[8,48,384]{2,1,0:T(8,128)(2,1)S(1)} %collective-permute-done.2.refs_4_) | copy-start | bytes 884740
  65.9 4.7 %collective-permute-start.6 = (bf16[8,192,384]{2,1,0:T(8,128)(2,1)S(1)}, bf16[8,192,384]{2,1,0:T(8,128)(2,1)S(1)}, u32[]{:S(2)}, u32[]{:S(2)}) collective-permute-start(bf16[8,192,384]{2,1,0:T(8,128)(2,1)S(1)} %get-tuple-element.43), channel_id=1, source_target_pairs={{0,8},{8,0},{1,9},{9,1},{2,10},{10,2},{3,11},{11,3},{4,12},{12,4},... | collective-permute-start | bytes 3538952 | tf_op jit(solution)/shard_map/ppermute | solution.py:273
  71.8 6.5 %collective-permute-start.3 = (bf16[8,48,384]{2,1,0:T(8,128)(2,1)S(1)}, bf16[8,48,384]{2,1,0:T(8,128)(2,1)S(1)}, u32[]{:S(2)}, u32[]{:S(2)}) collective-permute-start(bf16[8,48,384]{2,1,0:T(8,128)(2,1)S(1)} %collective-permute-done.refs_0_), channel_id=1, source_target_pairs={{0,8},{8,0},{1,9},{9,1},{2,10},{10,2},{3,11},{11,3},{4,12},{12,4},... | collective-permute-start | bytes 884744 | tf_op jit(solution)/shard_map/ppermute | solution.py:249
  73.8 4.4 %collective-permute-start.4 = (bf16[8,48,384]{2,1,0:T(8,128)(2,1)S(1)}, bf16[8,48,384]{2,1,0:T(8,128)(2,1)S(1)}, u32[]{:S(2)}, u32[]{:S(2)}) collective-permute-start(bf16[8,48,384]{2,1,0:T(8,128)(2,1)S(1)} %collective-permute-done.1.refs_2_), channel_id=1, source_target_pairs={{0,8},{8,0},{1,9},{9,1},{2,10},{10,2},{3,11},{11,3},{4,12},{12,4},... | collective-permute-start | bytes 884744 | tf_op jit(solution)/shard_map/ppermute | solution.py:249
  76.1 3.7 %collective-permute-start.5 = (bf16[8,48,384]{2,1,0:T(8,128)(2,1)}, bf16[8,48,384]{2,1,0:T(8,128)(2,1)S(1)}, u32[]{:S(2)}, u32[]{:S(2)}) collective-permute-start(bf16[8,48,384]{2,1,0:T(8,128)(2,1)} %copy-done.7), channel_id=1, source_target_pairs={{0,8},{8,0},{1,9},{9,1},{2,10},{10,2},{3,11},{11,3},{4,12},{12,4},... | collective-permute-start | bytes 884744 | tf_op jit(solution)/shard_map/ppermute | solution.py:249
  78.3 1.6 %copy-start.8 = (bf16[8,48,384]{2,1,0:T(8,128)(2,1)}, bf16[8,48,384]{2,1,0:T(8,128)(2,1)S(1)}, u32[]{:S(2)}) copy-start(bf16[8,48,384]{2,1,0:T(8,128)(2,1)S(1)} %collective-permute-done.3.refs_1_) | copy-start | bytes 884740
  78.3 1.6 %copy-start.9 = (bf16[8,48,384]{2,1,0:T(8,128)(2,1)}, bf16[8,48,384]{2,1,0:T(8,128)(2,1)S(1)}, u32[]{:S(2)}) copy-start(bf16[8,48,384]{2,1,0:T(8,128)(2,1)S(1)} %collective-permute-done.4.refs_3_) | copy-start | bytes 884740
  79.8 0.7 copy-start.10
Sparse Core Ops, SparseCore 0:
  10.1 45.0 all-gather.2
  71.9 49.3 reduce-scatter.1

commit v3 on v2

--- a/solution.py
+++ b/solution.py
@@ -26,7 +26,7 @@
 
 
 def params():
-    return pltpu.CompilerParams(vmem_limit_bytes=40 * 1024 * 1024)
+    return pltpu.CompilerParams(vmem_limit_bytes=16 * 1024 * 1024)
 
 
 def far(array):
@@ -70,37 +70,26 @@
     return weighted * (1.0 / jnp.sum(weighted, axis=1, keepdims=True))
 
 
-def forward_body(
-    lookup, core, queries, keys, values, got, grad_far,
-    probs, attn, keep, send,
-    key_set, value_set, grad, sems,
-):
+def attend_body(lookup, queries, keys, values, got, attn, key_set, value_set):
     frames, tokens, width = queries.shape
     heads, group_rows = width // HD, CF * tokens
-    chunks = grad.shape[0]
-    copies = [
-        pltpu.make_async_copy(grad_far.at[c], grad.at[c], sems.at[c]) for c in range(chunks)
-    ]
-    for copy in copies:
-        copy.start()
     for g in range(frames // CF):
         fill_sets(lookup, g, keys, values, got, key_set, value_set)
         for h in range(heads):
             cols = pl.ds(h * HD, HD)
             query = queries[pl.ds(g * CF, CF), :, cols].reshape(group_rows, HD)
-            prob = probabilities(query, key_set[:, cols])
-            probs[g * heads + h] = prob
+            low = probabilities(query, key_set[:, cols]).astype(BF)
             attn[pl.ds(g * group_rows, group_rows), cols] = dot(
-                prob.astype(BF), value_set[:, cols], NN
+                low, value_set[:, cols], NN
             ).astype(BF)
-    first = core[0] == 0
-    stripe = keep.shape[1]
-    for c, copy in enumerate(copies):
-        copy.wait()
-        term = dot(grad[c], attn[...], TN).astype(BF)
-        top, bottom = term[:stripe], term[stripe:]
-        keep[c] = jnp.where(first, top, bottom)
-        send[c] = jnp.where(first, bottom, top)
+
+
+def term_body(side, grad, attn, out):
+    stripe = out.shape[1]
+    first = side[0] == 0
+    for c in range(grad.shape[0]):
+        block = jnp.where(first, grad[c, :, :stripe], grad[c, :, stripe:])
+        out[c] = dot(block, attn[...], TN).astype(BF)
 
 
 def add_body(ours, theirs, out, total, sems):
@@ -114,13 +103,17 @@
         copy.wait()
 
 
+def join_body(*refs):
+    out = refs[-1]
+    for i, ref in enumerate(refs[:-1]):
+        out[i] = ref[...]
+
+
 def backward_body(
-    parts, lookup, place, queries, keys, values, got, probs, attn, grad_far, quarter, *refs
+    parts, lookup, place, queries, keys, values, got, attn, grad_far, quarter, halves, sibling,
+    query_grad, back, own_dk, own_dv,
+    key_sets, value_sets, probs, attn_grad, grad, weight, far_dk, far_dv, held_dk, held_dv, gsems, osems,
 ):
-    pieces, refs = refs[: 2 * (parts - 1)], refs[2 * (parts - 1) :]
-    query_grad, back, own_dk, own_dv = refs[:4]
-    key_set, value_set, attn_grad, grad, weight = refs[4:9]
-    far_dk, far_dv, held_dk, held_dv, gsems, wsems, osems = refs[9:]
     frames, tokens, width = queries.shape
     heads, group_rows = width // HD, CF * tokens
     chunks, _, chunk = grad.shape
@@ -128,29 +121,28 @@
     dp, core = place[0], place[1]
     half = shards // 2
 
-    copies = [
+    grad_copies = [
         pltpu.make_async_copy(grad_far.at[c], grad.at[c], gsems.at[c]) for c in range(chunks)
     ]
-    copies.append(
-        pltpu.make_async_copy(quarter.at[:, pl.ds(0, rows)], weight.at[:, dp], wsems.at[0])
-    )
-    for i, piece in enumerate(pieces):
-        origin = lax.rem(dp + parts - (1 + i // 2), parts)
-        side = core if i % 2 == 0 else 1 - core
-        copies.append(
-            pltpu.make_async_copy(
-                piece, weight.at[pl.ds(side * half, half), origin], wsems.at[1 + i]
-            )
-        )
-    for copy in copies:
+    for copy in grad_copies:
         copy.start()
+    for g in range(frames // CF):
+        fill_sets(lookup, g, keys, values, got, key_sets.at[g], value_sets.at[g])
+        for h in range(heads):
+            cols = pl.ds(h * HD, HD)
+            query = queries[pl.ds(g * CF, CF), :, cols].reshape(group_rows, HD)
+            probs[g * heads + h] = probabilities(query, key_sets[g, :, cols])
+    weight[:, dp] = quarter[:, :rows]
+    for i in range(parts - 1):
+        origin = lax.rem(dp + parts - (1 + i), parts)
+        weight[pl.ds(core * half, half), origin] = halves[i]
+        weight[pl.ds((1 - core) * half, half), origin] = sibling[i]
     far_dk[...] = jnp.zeros_like(far_dk)
     far_dv[...] = jnp.zeros_like(far_dv)
-    for copy in copies:
-        copy.wait()
     per_chunk = chunk // (parts * rows)
     total = None
-    for c in range(chunks):
+    for c, copy in enumerate(grad_copies):
+        copy.wait()
         block = weight[pl.ds(c * per_chunk, per_chunk)].reshape(chunk, width)
         term = dot(grad[c], block, NN)
         total = term if total is None else total + term
@@ -158,7 +150,6 @@
 
     copies = []
     for g in range(frames // CF):
-        fill_sets(lookup, g, keys, values, got, key_set, value_set)
         mine = pl.ds(g * group_rows, group_rows)
         for h in range(heads):
             cols = pl.ds(h * HD, HD)
@@ -168,9 +159,9 @@
             row_dot = jnp.sum(
                 out_grad.astype(F32) * attn[mine, cols].astype(F32), axis=1, keepdims=True
             )
-            prob_grad = dot(out_grad, value_set[:, cols], NT)
+            prob_grad = dot(out_grad, value_sets[g, :, cols], NT)
             score_grad = (prob * (prob_grad - row_dot)).astype(BF)
-            dq = (dot(score_grad, key_set[:, cols], NN) * (HD**-0.5)).astype(BF)
+            dq = (dot(score_grad, key_sets[g, :, cols], NN) * (HD**-0.5)).astype(BF)
             query_grad[pl.ds(g * CF, CF), :, cols] = dq.reshape(CF, tokens, HD)
             dk = dot(score_grad, query, TN) * (HD**-0.5)
             dv = dot(prob.astype(BF), out_grad, TN)
@@ -243,33 +234,35 @@
         lax.ppermute(mine, "dp", [(i, (i + s) % parts) for i in range(parts)])
         for s in range(1, parts)
     ]
-    got, *halves = lax.optimization_barrier((got, *halves))
-    pieces = []
-    for piece in halves:
-        pieces += [piece, lax.ppermute(piece, "core", other)]
-
     partial = shape((heads, stripe, width), BF)
     key_rows = (CF + RET) * tokens
     sets = pltpu.VMEM((key_rows, width), BF)
-    chunks = pltpu.VMEM((heads, rows, width), BF)
     token_sum = pltpu.VMEM((rows, width), F32)
     far_sum = pltpu.VMEM((shards, tokens, width), F32)
-    probs, attn, keep, send = pl.pallas_call(
-        forward_body,
-        out_shape=(
-            shape((groups * width // HD, CF * tokens, key_rows), F32),
-            shape((rows, width), BF),
-            partial,
-            partial,
-        ),
-        in_specs=[SMEM] * 2 + [VMEM] * 4 + [HBM],
-        out_specs=(VMEM,) * 4,
-        scratch_shapes=[sets, sets, chunks, dma((heads,))],
-        compiler_params=params(),
-        cost_estimate=cost(4 * 10**9, 8 * 10**6),
-        name="forward",
-    )(lookup, core[None], queries, keys, values, got, far(grad))
-
+    attn = pl.pallas_call(
+        attend_body,
+        out_shape=shape((rows, width), BF),
+        in_specs=[SMEM] + [VMEM] * 4,
+        out_specs=VMEM,
+        scratch_shapes=[sets, sets],
+        compiler_params=params(),
+        cost_estimate=cost(2 * 10**9, 8 * 10**6),
+        name="attend",
+    )(lookup, queries, keys, values, got)
+    attn, *halves = lax.optimization_barrier((attn, *halves))
+
+    def term(side, name):
+        return pl.pallas_call(
+            term_body,
+            out_shape=partial,
+            in_specs=[SMEM, VMEM, VMEM],
+            out_specs=VMEM,
+            compiler_params=params(),
+            cost_estimate=cost(3 * 10**9, 3 * 10**6),
+            name=name,
+        )(side[None], grad, attn)
+
+    send, keep = term(1 - core, "send"), term(core, "keep")
     theirs = lax.ppermute(send, "core", other)
     chip_sum = pl.pallas_call(
         add_body,
@@ -281,6 +274,16 @@
         cost_estimate=cost(10**6, 4 * 10**6),
         name="add",
     )(keep, theirs)
+    halves = pl.pallas_call(
+        join_body,
+        out_shape=shape((parts - 1, half, part_rows, width), BF),
+        in_specs=[VMEM] * (parts - 1),
+        out_specs=VMEM,
+        compiler_params=params(),
+        cost_estimate=cost(0, 2 * 10**6),
+        name="join",
+    )(*halves)
+    sibling = lax.ppermute(halves, "core", other)
     weight_grad = lax.psum_scatter(chip_sum, "y", scatter_dimension=0, tiled=False)
 
     query_grad, back, own_dk, own_dv = pl.pallas_call(
@@ -291,28 +294,28 @@
             shape((rows, width), F32),
             shape((rows, width), F32),
         ),
-        in_specs=[SMEM] * 2 + [VMEM] * 6 + [HBM] * (2 + len(pieces)),
+        in_specs=[SMEM] * 2 + [VMEM] * 5 + [HBM] + [VMEM] * 3,
         out_specs=(VMEM, VMEM, HBM, HBM),
         scratch_shapes=[
-            sets,
-            sets,
+            pltpu.VMEM((groups, key_rows, width), BF),
+            pltpu.VMEM((groups, key_rows, width), BF),
+            pltpu.VMEM((groups * width // HD, CF * tokens, key_rows), F32),
             pltpu.VMEM((rows, width), BF),
-            chunks,
+            pltpu.VMEM((heads, rows, width), BF),
             pltpu.VMEM((shards, parts, part_rows, width), BF),
             far_sum,
             far_sum,
             token_sum,
             token_sum,
             dma((heads,)),
-            dma((1 + len(pieces),)),
             dma((groups, 2)),
         ],
         compiler_params=params(),
         cost_estimate=cost(6 * 10**9, 9 * 10**6),
         name="backward",
     )(
-        lookup, jnp.stack([dp, core]), queries, keys, values, got, probs, attn,
-        far(grad), far(quarter), *[far(p) for p in pieces],
+        lookup, jnp.stack([dp, core]), queries, keys, values, got, attn,
+        far(grad), quarter, halves, sibling,
     )
     came = lax.all_to_all(back, time, split_axis=0, concat_axis=0, tiled=True)
 

time: 134 us -> 131 us (0.978)
  starting transfers between devices: 21.1 us -> 17.1 us
  local copies, waits for them, and re-layouts: 0.97 us -> 3.48 us
  blocking collectives: 58.2 us -> 55.9 us
    ppermute x3, waiting for transfers between devices: 10.9 us -> 0.01 us  [per_device(): lax.ppermute(mine, 'dp', [(i, (i + s) % parts) for i in range(parts)])]
    all_to_all x1, waiting for transfers between devices: 2.57 us -> 12.8 us  [per_device(): got = lax.all_to_all(packed, time, split_axis=0, concat_axis=0, tiled=True)]
    reduce_scatter x1, waiting for transfers between devices: 0.01 us -> 5.22 us  [per_device(): lax.psum_scatter(chip_sum, 'y', scatter_dimension=0, tiled=False)]
    ppermute x3 -> x1, starting transfers between devices: 6.37 us -> 2.41 us  [per_device(): sibling = lax.ppermute(halves, 'core', other)]
    ppermute x1, waiting for transfers between devices: 2.81 us -> 0.01 us  [per_device(): theirs = lax.ppermute(send, 'core', other)]
    all_to_all x1, blocking collectives: 34.6 us -> 32.3 us  [per_device(): came = lax.all_to_all(back, time, split_axis=0, concat_axis=0, tiled=True)]
    unnamed x24, local copies, waits for them, and re-layouts: 0.76 us -> 2.55 us
    ppermute x3 -> x1, waiting for transfers between devices: 1.54 us -> 0.01 us  [per_device(): sibling = lax.ppermute(halves, 'core', other)]
  transfers between devices with their start and end apart: 10 -> 8, of which waited for: 6 -> 2; matrix products, arithmetic and copies ran while one was open for 1% -> 1% of each run, Pallas kernels for 8% -> 12%
where the time goes in v3:
time: 131 us; the launch traced here: 130 us
  blocking collectives  55.9 us (43%)
  waiting for transfers between devices  18.7 us (14%)
  Pallas kernels  17.4 us (13%)
  starting transfers between devices  17.1 us (13%)
  between operations  14.3 us (11%)
  local copies, waits for them, and re-layouts  3.48 us (3%)
  other arithmetic  2.56 us (2%)
    all_to_all x1, blocking collectives, per_device(): came = lax.all_to_all(back, time, split_axis=0, concat_axis=0, tiled=True)  32.3 us
    all_gather x1, blocking collectives, per_device(): lax.all_gather(jnp.concatenate([part, names], axis=0), time, axis=0, tile...  23.6 us
    all_to_all x1, waiting for transfers between devices, per_device(): got = lax.all_to_all(packed, time, split_axis=0, concat_axis=0, tiled=True)  12.8 us
    ppermute x3, starting transfers between devices, per_device(): lax.ppermute(mine, 'dp', [(i, (i + s) % parts) for i in range(parts)])  9.01 us
    pallas_call x1, Pallas kernels, per_device(): pl.pallas_call(functools.partial(backward_body, parts), out_shape=(shape(...  7.69 us
    reduce_scatter x1, waiting for transfers between devices, per_device(): lax.psum_scatter(chip_sum, 'y', scatter_dimension=0, tiled=False)  5.22 us
    all_to_all x1, starting transfers between devices, per_device(): got = lax.all_to_all(packed, time, split_axis=0, concat_axis=0, tiled=True)  3.71 us
    pallas_call x1, Pallas kernels, per_device(): pl.pallas_call(attend_body, out_shape=shape((rows, width), BF), in_specs=...  2.73 us
  transfers between devices with their start and end apart: 8, of which 2 were waited for; matrix products, arithmetic and copies ran while one was open for 1% of the time, Pallas kernels for 12%

profile of v3, /device:TPU:1, one launch (start us, length us, event | category | flops | bytes accessed | tf_op | source)
XLA Modules:
  0.0 129.5 jit_solution(15190591905826300067)
XLA Ops:
  7.2 0.7 all-gather.3.cloned.1.call-update
  7.9 0.7 convert_element_type.23
  8.7 23.6 %all-gather = bf16[1024,384]{1,0:T(8,128)(2,1)S(1)} all-gather(bf16[64,384]{1,0:T(8,128)(2,1)S(1)} %fusion.1), channel_id=2, replica_groups=mesh['dp'=4,'y'=8,'core'=2,'head'=8] {'y','core'}, dimensions={0}, use_global_device_ids=true | all-gather | bytes 835584 | tf_op jit(solution)/shard_map/all_gather | solution.py:215
  32.3 0.1 fusion.4.source
  32.5 1.7 %pack.1 = bf16[16,2,32,384]{3,2,1,0:T(8,128)(2,1)} custom-call(s32[16]{0:T(128)S(1)} %fusion.4.source, bf16[8,32,384]{2,1,0:T(8,128)(2,1)S(1)} %copy-done.1, bf16[8,32,384]{2,1,0:T(8,128)(2,1)S(1)} %copy-done.3), custom_call_target="tpu_custom_call" | custom-call | bytes 1572864 | tf_op jit(solution)/shard_map/pack/pallas_call | solution.py:220
  34.2 3.7 %all-to-all-start = ((bf16[16,2,32,384]{3,2,1,0:T(8,128)(2,1)}), bf16[16,2,32,384]{3,2,1,0:T(8,128)(2,1)S(1)}, u32[]{:S(2)}, u32[]{:S(2)}) async-start(bf16[16,2,32,384]{3,2,1,0:T(8,128)(2,1)} %pack.1), calls=%async_computation | async-start | bytes 1572864 | tf_op jit(solution)/shard_map/all_to_all | solution.py:230
  37.9 0.8 constant_dynamic-slice_fusion
  38.7 1.9 %collective-permute-start = (bf16[8,48,384]{2,1,0:T(8,128)(2,1)}, bf16[8,48,384]{2,1,0:T(8,128)(2,1)S(1)}, u32[]{:S(2)}, u32[]{:S(2)}) collective-permute-start(bf16[8,48,384]{2,1,0:T(8,128)(2,1)} %constant_dynamic-slice_fusion), channel_id=1, source_target_pairs={{0,128},{128,256},{256,384},{384,0},{1,129},{129,257},{257,385},{3... | collective-permute-start | bytes 884744 | tf_op jit(solution)/shard_map/ppermute | solution.py:234
  40.6 4.0 %collective-permute-start.1 = (bf16[8,48,384]{2,1,0:T(8,128)(2,1)}, bf16[8,48,384]{2,1,0:T(8,128)(2,1)S(1)}, u32[]{:S(2)}, u32[]{:S(2)}) collective-permute-start(bf16[8,48,384]{2,1,0:T(8,128)(2,1)} %constant_dynamic-slice_fusion), channel_id=1, source_target_pairs={{0,256},{128,384},{256,0},{384,128},{1,257},{129,385},{257,1},{385... | collective-permute-start | bytes 884744 | tf_op jit(solution)/shard_map/ppermute | solution.py:234
  44.7 3.1 %collective-permute-start.2 = (bf16[8,48,384]{2,1,0:T(8,128)(2,1)}, bf16[8,48,384]{2,1,0:T(8,128)(2,1)S(1)}, u32[]{:S(2)}, u32[]{:S(2)}) collective-permute-start(bf16[8,48,384]{2,1,0:T(8,128)(2,1)} %constant_dynamic-slice_fusion), channel_id=1, source_target_pairs={{0,384},{128,0},{256,128},{384,256},{1,385},{129,1},{257,129},{385... | collective-permute-start | bytes 884744 | tf_op jit(solution)/shard_map/ppermute | solution.py:234
  47.8 12.8 %all-to-all-done.got = bf16[16,2,32,384]{3,2,1,0:T(8,128)(2,1)S(1)} async-done(((bf16[16,2,32,384]{3,2,1,0:T(8,128)(2,1)}), bf16[16,2,32,384]{3,2,1,0:T(8,128)(2,1)S(1)}, u32[]{:S(2)}, u32[]{:S(2)}) %all-to-all-start) | async-done | bytes 786464 | tf_op jit(solution)/shard_map/all_to_all | solution.py:230
  60.6 2.7 %attend.1.attn = bf16[256,384]{1,0:T(8,128)(2,1)S(1)} custom-call(s32[16]{0:T(128)S(1)} %and_select_fusion.lookup, bf16[8,32,384]{2,1,0:T(8,128)(2,1)S(1)} %copy-done.6, bf16[8,32,384]{2,1,0:T(8,128)(2,1)S(1)} %copy-done.1, bf16[8,32,384]{2,1,0:T(8,128)(2,1)S(1)} %copy-done.3, bf16[16,2,32,384]{3,2,1,0:T(8,128)(2,1)S(1)} %all-to-all-done.got), custom_call_target="tpu_custom_call" | custom-call | flops 2000000000 | bytes 8000000 | tf_op jit(solution)/shard_map/attend/pallas_call | solution.py:242
  63.4 1.4 %copy-done.5 = bf16[8,256,384]{2,1,0:T(8,128)(2,1)S(1)} copy-done((bf16[8,256,384]{2,1,0:T(8,128)(2,1)S(1)}, bf16[8,256,384]{2,1,0:T(8,128)(2,1)}, u32[]{:S(2)}) %copy-start.5) | copy-done | bytes 1572888
  64.8 1.3 %send.1 = bf16[8,192,384]{2,1,0:T(8,128)(2,1)S(1)} custom-call(s32[1]{0:T(128)} %bitcast.5.side, bf16[8,256,384]{2,1,0:T(8,128)(2,1)S(1)} %copy-done.5, bf16[256,384]{1,0:T(8,128)(2,1)S(1)} %attend.1.attn), custom_call_target="tpu_custom_call" | custom-call | flops 3000000000 | bytes 3000000 | tf_op jit(solution)/shard_map/send/pallas_call | solution.py:255
  66.2 1.9 %collective-permute-start.4 = (bf16[8,192,384]{2,1,0:T(8,128)(2,1)S(1)}, bf16[8,192,384]{2,1,0:T(8,128)(2,1)S(1)}, u32[]{:S(2)}, u32[]{:S(2)}) collective-permute-start(bf16[8,192,384]{2,1,0:T(8,128)(2,1)S(1)} %send.1), channel_id=1, source_target_pairs={{0,8},{8,0},{1,9},{9,1},{2,10},{10,2},{3,11},{11,3},{4,12},{12,4},... | collective-permute-start | bytes 3538952 | tf_op jit(solution)/shard_map/ppermute | solution.py:266
  68.2 2.4 %collective-permute-start.3 = (bf16[3,8,48,384]{3,2,1,0:T(8,128)(2,1)S(1)}, bf16[3,8,48,384]{3,2,1,0:T(8,128)(2,1)}, u32[]{:S(2)}, u32[]{:S(2)}) collective-permute-start(bf16[3,8,48,384]{3,2,1,0:T(8,128)(2,1)S(1)} %join.1.halves), channel_id=1, source_target_pairs={{0,8},{8,0},{1,9},{9,1},{2,10},{10,2},{3,11},{11,3},{4,12},{12,4},... | collective-permute-start | bytes 2654216 | tf_op jit(solution)/shard_map/ppermute | solution.py:286
  70.6 1.3 %keep.1.ours = bf16[8,192,384]{2,1,0:T(8,128)(2,1)S(1)} custom-call(s32[1]{0:T(128)} %bitcast.1.side, bf16[8,256,384]{2,1,0:T(8,128)(2,1)S(1)} %copy-done.5, bf16[256,384]{1,0:T(8,128)(2,1)S(1)} %copy-done.9), custom_call_target="tpu_custom_call" | custom-call | flops 3000000000 | bytes 3000000 | tf_op jit(solution)/shard_map/keep/pallas_call | solution.py:255
  71.9 1.1 add.36
  73.2 0.8 copy-done.2
  74.3 7.7 %backward.1 = (bf16[8,32,384]{2,1,0:T(8,128)(2,1)}, bf16[16,2,32,384]{3,2,1,0:T(8,128)(2,1)S(1)}, f32[256,384]{1,0:T(8,128)S(1)}, f32[256,384]{1,0:T(8,128)S(1)}) custom-call(s32[16]{0:T(128)S(1)} %and_select_fusion.lookup, s32[2]{0:T(128)S(1)} %pad_add_fusion.place, bf16[8,32,384]{2,1,0:T(8,128)(2,1)S(1)} %copy-done.7, bf16[8,32,384]{2,1,0:T(8,128)(2,1)S(1)} %copy-done.2, ...), custom_call_target="tpu_custom_call" | custom-call | flops 6000000000 | bytes 9000000 | tf_op jit(solution)/shard_map/backward/pallas_call | solution.py:289
  82.0 32.3 %all_to_all.10.came = bf16[16,2,32,384]{3,2,1,0:T(8,128)(2,1)S(1)} all-to-all(bf16[16,2,32,384]{3,2,1,0:T(8,128)(2,1)S(1)} %get-tuple-element.31), channel_id=1, replica_groups=mesh['dp'=4,'y'=8,'core'=2,'head'=8] {'y','core'}, dimensions={0} | all-to-all | bytes 1572864 | tf_op jit(solution)/shard_map/all_to_all | solution.py:320
  114.3 1.5 %finish.1 = (bf16[8,32,384]{2,1,0:T(8,128)(2,1)}, bf16[8,32,384]{2,1,0:T(8,128)(2,1)}) custom-call(s32[16]{0:T(128)S(1)} %fusion.4.source, bf16[16,2,32,384]{3,2,1,0:T(8,128)(2,1)S(1)} %all_to_all.10.came, f32[256,384]{1,0:T(8,128)S(1)} %get-tuple-element.32.own_dk, f32[256,384]{1,0:T(8,128)S(1)} %get-tuple-element.33.own_dv), custom_call_target="tpu_custom_call" | custom-call | flops 1000000 | bytes 3000000 | tf_op jit(solution)/shard_map/finish/pallas_call | solution.py:322
  115.8 5.2 %reduce-scatter.2.cloned.1.call-done = bf16[1,192,384]{2,1,0:T(8,128)(2,1)} async-done(((bf16[8,192,384]{2,1,0:T(8,128)(2,1)}), bf16[1,192,384]{2,1,0:T(8,128)(2,1)}) %reduce-scatter.2.cloned.1.call-update) | async-done | bytes 147472 | tf_op jit(solution)/shard_map/reduce_scatter | solution.py:287
  121.0 1.6 %bitcast_convert_fusion = f32[192,384]{1,0:T(8,128)} fusion(bf16[1,192,384]{2,1,0:T(8,128)(2,1)} %reduce-scatter.2.cloned.1.call-done), kind=kLoop, calls=%fused_computation | loop fusion | flops 73728 | bytes 442368 | tf_op jit(solution)/shard_map/convert_element_type | solution.py:332
  (39 shorter events, 0.8 us)
Async XLA Ops:
  7.2 1.6 %copy-start = (bf16[192,384]{1,0:T(8,128)(2,1)S(1)}, bf16[192,384]{1,0:T(8,128)(2,1)}, u32[]{:S(2)}) copy-start(bf16[192,384]{1,0:T(8,128)(2,1)} %param.12) | copy-start | bytes 442372
  7.2 25.3 %copy-start.1 = (bf16[8,32,384]{2,1,0:T(8,128)(2,1)S(1)}, bf16[8,32,384]{2,1,0:T(8,128)(2,1)}, u32[]{:S(2)}) copy-start(bf16[8,32,384]{2,1,0:T(8,128)(2,1)} %keys.5) | copy-start | bytes 589828
  7.2 25.3 %copy-start.3 = (bf16[8,32,384]{2,1,0:T(8,128)(2,1)S(1)}, bf16[8,32,384]{2,1,0:T(8,128)(2,1)}, u32[]{:S(2)}) copy-start(bf16[8,32,384]{2,1,0:T(8,128)(2,1)} %values.5) | copy-start | bytes 589828
  7.2 56.2 %all-gather.3.cloned.1.call-start = ((), (), s32[]{:S(2)}) async-start(), calls=%async_computation.3 | async-start | bytes 1769472 | tf_op jit(solution)/shard_map/all_gather | solution.py:211
  34.2 13.6 %copy-start.11 = (s32[2,8]{1,0:T(2,128)S(1)}, s32[2,8]{1,0:T(2,128)}, u32[]{:S(2)}) copy-start(s32[2,8]{1,0:T(2,128)} %param.13) | copy-start | bytes 196
  34.2 26.4 %copy-start.6 = (bf16[8,32,384]{2,1,0:T(8,128)(2,1)S(1)}, bf16[8,32,384]{2,1,0:T(8,128)(2,1)}, u32[]{:S(2)}) copy-start(bf16[8,32,384]{2,1,0:T(8,128)(2,1)} %queries.3) | copy-start | bytes 589828
  34.2 26.4 %all-to-all-start = ((bf16[16,2,32,384]{3,2,1,0:T(8,128)(2,1)}), bf16[16,2,32,384]{3,2,1,0:T(8,128)(2,1)S(1)}, u32[]{:S(2)}, u32[]{:S(2)}) async-start(bf16[16,2,32,384]{3,2,1,0:T(8,128)(2,1)} %pack.1), calls=%async_computation | async-start | bytes 1572864 | tf_op jit(solution)/shard_map/all_to_all | solution.py:230
  37.9 83.1 %reduce-scatter.2.cloned.1.call-start = ((), (), s32[]{:S(2)}) async-start(), calls=%async_computation.4 | async-start | bytes 1327104 | tf_op jit(solution)/shard_map/reduce_scatter | solution.py:287
  38.7 24.7 %collective-permute-start = (bf16[8,48,384]{2,1,0:T(8,128)(2,1)}, bf16[8,48,384]{2,1,0:T(8,128)(2,1)S(1)}, u32[]{:S(2)}, u32[]{:S(2)}) collective-permute-start(bf16[8,48,384]{2,1,0:T(8,128)(2,1)} %constant_dynamic-slice_fusion), channel_id=1, source_target_pairs={{0,128},{128,256},{256,384},{384,0},{1,129},{129,257},{257,385},{3... | collective-permute-start | bytes 884744 | tf_op jit(solution)/shard_map/ppermute | solution.py:234
  40.6 22.8 %collective-permute-start.1 = (bf16[8,48,384]{2,1,0:T(8,128)(2,1)}, bf16[8,48,384]{2,1,0:T(8,128)(2,1)S(1)}, u32[]{:S(2)}, u32[]{:S(2)}) collective-permute-start(bf16[8,48,384]{2,1,0:T(8,128)(2,1)} %constant_dynamic-slice_fusion), channel_id=1, source_target_pairs={{0,256},{128,384},{256,0},{384,128},{1,257},{129,385},{257,1},{385... | collective-permute-start | bytes 884744 | tf_op jit(solution)/shard_map/ppermute | solution.py:234
  44.7 18.7 %collective-permute-start.2 = (bf16[8,48,384]{2,1,0:T(8,128)(2,1)}, bf16[8,48,384]{2,1,0:T(8,128)(2,1)S(1)}, u32[]{:S(2)}, u32[]{:S(2)}) collective-permute-start(bf16[8,48,384]{2,1,0:T(8,128)(2,1)} %constant_dynamic-slice_fusion), channel_id=1, source_target_pairs={{0,384},{128,0},{256,128},{384,256},{1,385},{129,1},{257,129},{385... | collective-permute-start | bytes 884744 | tf_op jit(solution)/shard_map/ppermute | solution.py:234
  63.3 2.8 %copy-start.8 = (bf16[256,384]{1,0:T(8,128)(2,1)}, bf16[256,384]{1,0:T(8,128)(2,1)S(1)}, u32[]{:S(2)}) copy-start(bf16[256,384]{1,0:T(8,128)(2,1)S(1)} %attend.1.attn) | copy-start | bytes 589828
  63.4 1.4 %copy-start.5 = (bf16[8,256,384]{2,1,0:T(8,128)(2,1)S(1)}, bf16[8,256,384]{2,1,0:T(8,128)(2,1)}, u32[]{:S(2)}) copy-start(bf16[8,256,384]{2,1,0:T(8,128)(2,1)} %all-gather.3.cloned.1.call-done.grad_far.grad) | copy-start | bytes 4718596
  66.2 5.8 %collective-permute-start.4 = (bf16[8,192,384]{2,1,0:T(8,128)(2,1)S(1)}, bf16[8,192,384]{2,1,0:T(8,128)(2,1)S(1)}, u32[]{:S(2)}, u32[]{:S(2)}) collective-permute-start(bf16[8,192,384]{2,1,0:T(8,128)(2,1)S(1)} %send.1), channel_id=1, source_target_pairs={{0,8},{8,0},{1,9},{9,1},{2,10},{10,2},{3,11},{11,3},{4,12},{12,4},... | collective-permute-start | bytes 3538952 | tf_op jit(solution)/shard_map/ppermute | solution.py:266
  68.1 2.5 %copy-start.9 = (bf16[256,384]{1,0:T(8,128)(2,1)S(1)}, bf16[256,384]{1,0:T(8,128)(2,1)}, u32[]{:S(2)}) copy-start(bf16[256,384]{1,0:T(8,128)(2,1)} %copy-done.8) | copy-start | bytes 589828
  68.2 5.1 %collective-permute-start.3 = (bf16[3,8,48,384]{3,2,1,0:T(8,128)(2,1)S(1)}, bf16[3,8,48,384]{3,2,1,0:T(8,128)(2,1)}, u32[]{:S(2)}, u32[]{:S(2)}) collective-permute-start(bf16[3,8,48,384]{3,2,1,0:T(8,128)(2,1)S(1)} %join.1.halves), channel_id=1, source_target_pairs={{0,8},{8,0},{1,9},{9,1},{2,10},{10,2},{3,11},{11,3},{4,12},{12,4},... | collective-permute-start | bytes 2654216 | tf_op jit(solution)/shard_map/ppermute | solution.py:286
  73.1 0.9 copy-start.2
  73.1 1.0 copy-start.4
  73.1 1.1 copy-start.7
  73.1 1.2 copy-start.10
Sparse Core Ops, SparseCore 0:
  10.1 45.0 all-gather.2
  73.3 47.7 reduce-scatter.1

commit v4 on v3

--- a/solution.py
+++ b/solution.py
@@ -70,17 +70,17 @@
     return weighted * (1.0 / jnp.sum(weighted, axis=1, keepdims=True))
 
 
-def attend_body(lookup, queries, keys, values, got, attn, key_set, value_set):
+def attend_body(lookup, queries, keys, values, got, attn, key_sets, value_sets):
     frames, tokens, width = queries.shape
     heads, group_rows = width // HD, CF * tokens
     for g in range(frames // CF):
-        fill_sets(lookup, g, keys, values, got, key_set, value_set)
+        fill_sets(lookup, g, keys, values, got, key_sets.at[g], value_sets.at[g])
         for h in range(heads):
             cols = pl.ds(h * HD, HD)
             query = queries[pl.ds(g * CF, CF), :, cols].reshape(group_rows, HD)
-            low = probabilities(query, key_set[:, cols]).astype(BF)
+            low = probabilities(query, key_sets[g, :, cols]).astype(BF)
             attn[pl.ds(g * group_rows, group_rows), cols] = dot(
-                low, value_set[:, cols], NN
+                low, value_sets[g, :, cols], NN
             ).astype(BF)
 
 
@@ -220,7 +220,7 @@
     packed = pl.pallas_call(
         pack_body,
         out_shape=shape((shards, 2, tokens, width), BF),
-        in_specs=[SMEM, HBM, HBM],
+        in_specs=[SMEM, VMEM, VMEM],
         out_specs=HBM,
         scratch_shapes=[dma((shards, 2))],
         compiler_params=params(),
@@ -234,9 +234,10 @@
         lax.ppermute(mine, "dp", [(i, (i + s) % parts) for i in range(parts)])
         for s in range(1, parts)
     ]
+    got, grad = lax.optimization_barrier((got, grad))
     partial = shape((heads, stripe, width), BF)
     key_rows = (CF + RET) * tokens
-    sets = pltpu.VMEM((key_rows, width), BF)
+    sets = pltpu.VMEM((groups, key_rows, width), BF)
     token_sum = pltpu.VMEM((rows, width), F32)
     far_sum = pltpu.VMEM((shards, tokens, width), F32)
     attn = pl.pallas_call(
@@ -297,8 +298,8 @@
         in_specs=[SMEM] * 2 + [VMEM] * 5 + [HBM] + [VMEM] * 3,
         out_specs=(VMEM, VMEM, HBM, HBM),
         scratch_shapes=[
-            pltpu.VMEM((groups, key_rows, width), BF),
-            pltpu.VMEM((groups, key_rows, width), BF),
+            sets,
+            sets,
             pltpu.VMEM((groups * width // HD, CF * tokens, key_rows), F32),
             pltpu.VMEM((rows, width), BF),
             pltpu.VMEM((heads, rows, width), BF),

time: 131 us -> 129 us (0.985)
  local copies, waits for them, and re-layouts: 3.48 us -> 1.34 us
  waiting for transfers between devices: 18.7 us -> 16.7 us
  blocking collectives: 55.9 us -> 57.6 us
    reduce_scatter x1, waiting for transfers between devices: 5.22 us -> 2.51 us  [per_device(): lax.psum_scatter(chip_sum, 'y', scatter_dimension=0, tiled=False)]
    all_to_all x1, blocking collectives: 32.3 us -> 34 us  [per_device(): came = lax.all_to_all(back, time, split_axis=0, concat_axis=0, tiled=True)]
    unnamed x24 -> x22, local copies, waits for them, and re-layouts: 2.55 us -> 1.13 us
  transfers between devices with their start and end apart: 8 -> 8, of which waited for: 2 -> 2; matrix products, arithmetic and copies ran while one was open for 1% -> 1% of each run, Pallas kernels for 12% -> 13%
where the time goes in v4:
time: 129 us; the launch traced here: 127 us
  blocking collectives  57.6 us (45%)
  Pallas kernels  17.4 us (13%)
  starting transfers between devices  17.1 us (13%)
  waiting for transfers between devices  16.7 us (13%)
  between operations  14.3 us (11%)
  other arithmetic  2.56 us (2%)
  local copies, waits for them, and re-layouts  1.34 us (1%)
    all_to_all x1, blocking collectives, per_device(): came = lax.all_to_all(back, time, split_axis=0, concat_axis=0, tiled=True)  34 us
    all_gather x1, blocking collectives, per_device(): lax.all_gather(jnp.concatenate([part, names], axis=0), time, axis=0, tile...  23.6 us
    all_to_all x1, waiting for transfers between devices, per_device(): got = lax.all_to_all(packed, time, split_axis=0, concat_axis=0, tiled=True)  13.5 us
    ppermute x3, starting transfers between devices, per_device(): lax.ppermute(mine, 'dp', [(i, (i + s) % parts) for i in range(parts)])  9.02 us
    pallas_call x1, Pallas kernels, per_device(): pl.pallas_call(functools.partial(backward_body, parts), out_shape=(shape(...  7.68 us
    all_to_all x1, starting transfers between devices, per_device(): got = lax.all_to_all(packed, time, split_axis=0, concat_axis=0, tiled=True)  3.71 us
    pallas_call x1, Pallas kernels, per_device(): pl.pallas_call(attend_body, out_shape=shape((rows, width), BF), in_specs=...  2.72 us
    pallas_call x2, Pallas kernels, term(): pl.pallas_call(term_body, out_shape=partial, in_specs=[SMEM, VMEM, VMEM],...  2.61 us
  transfers between devices with their start and end apart: 8, of which 2 were waited for; matrix products, arithmetic and copies ran while one was open for 1% of the time, Pallas kernels for 13%

profile of v4, /device:TPU:1, one launch (start us, length us, event | category | flops | bytes accessed | tf_op | source)
XLA Modules:
  0.0 127.0 jit_solution(18369241597181005353)
XLA Ops:
  7.2 0.7 all-gather.3.cloned.1.call-update
  7.9 0.7 convert_element_type.23
  8.7 23.6 %all-gather = bf16[1024,384]{1,0:T(8,128)(2,1)S(1)} all-gather(bf16[64,384]{1,0:T(8,128)(2,1)S(1)} %fusion.1), channel_id=2, replica_groups=mesh['dp'=4,'y'=8,'core'=2,'head'=8] {'y','core'}, dimensions={0}, use_global_device_ids=true | all-gather | bytes 835584 | tf_op jit(solution)/shard_map/all_gather | solution.py:215
  32.3 0.1 fusion.4.source
  32.5 1.7 %pack.1 = bf16[16,2,32,384]{3,2,1,0:T(8,128)(2,1)} custom-call(s32[16]{0:T(128)S(1)} %fusion.4.source, bf16[8,32,384]{2,1,0:T(8,128)(2,1)S(1)} %copy-done.1, bf16[8,32,384]{2,1,0:T(8,128)(2,1)S(1)} %copy-done.3), custom_call_target="tpu_custom_call" | custom-call | bytes 1572864 | tf_op jit(solution)/shard_map/pack/pallas_call | solution.py:220
  34.2 3.7 %all-to-all-start = ((bf16[16,2,32,384]{3,2,1,0:T(8,128)(2,1)}), bf16[16,2,32,384]{3,2,1,0:T(8,128)(2,1)S(1)}, u32[]{:S(2)}, u32[]{:S(2)}) async-start(bf16[16,2,32,384]{3,2,1,0:T(8,128)(2,1)} %pack.1), calls=%async_computation | async-start | bytes 1572864 | tf_op jit(solution)/shard_map/all_to_all | solution.py:230
  38.0 1.9 %collective-permute-start = (bf16[8,48,384]{2,1,0:T(8,128)(2,1)S(1)}, bf16[8,48,384]{2,1,0:T(8,128)(2,1)S(1)}, u32[]{:S(2)}, u32[]{:S(2)}) collective-permute-start(bf16[8,48,384]{2,1,0:T(8,128)(2,1)S(1)} %constant_dynamic-slice_fusion), channel_id=1, source_target_pairs={{0,128},{128,256},{256,384},{384,0},{1,129},{129,257},{257,385},{3... | collective-permute-start | bytes 884744 | tf_op jit(solution)/shard_map/ppermute | solution.py:234
  39.9 4.0 %collective-permute-start.1 = (bf16[8,48,384]{2,1,0:T(8,128)(2,1)S(1)}, bf16[8,48,384]{2,1,0:T(8,128)(2,1)S(1)}, u32[]{:S(2)}, u32[]{:S(2)}) collective-permute-start(bf16[8,48,384]{2,1,0:T(8,128)(2,1)S(1)} %constant_dynamic-slice_fusion), channel_id=1, source_target_pairs={{0,256},{128,384},{256,0},{384,128},{1,257},{129,385},{257,1},{385... | collective-permute-start | bytes 884744 | tf_op jit(solution)/shard_map/ppermute | solution.py:234
  44.0 3.1 %collective-permute-start.2 = (bf16[8,48,384]{2,1,0:T(8,128)(2,1)S(1)}, bf16[8,48,384]{2,1,0:T(8,128)(2,1)S(1)}, u32[]{:S(2)}, u32[]{:S(2)}) collective-permute-start(bf16[8,48,384]{2,1,0:T(8,128)(2,1)S(1)} %constant_dynamic-slice_fusion), channel_id=1, source_target_pairs={{0,384},{128,0},{256,128},{384,256},{1,385},{129,1},{257,129},{385... | collective-permute-start | bytes 884744 | tf_op jit(solution)/shard_map/ppermute | solution.py:234
  47.1 13.5 %all-to-all-done.got = bf16[16,2,32,384]{3,2,1,0:T(8,128)(2,1)S(1)} async-done(((bf16[16,2,32,384]{3,2,1,0:T(8,128)(2,1)}), bf16[16,2,32,384]{3,2,1,0:T(8,128)(2,1)S(1)}, u32[]{:S(2)}, u32[]{:S(2)}) %all-to-all-start) | async-done | bytes 786464 | tf_op jit(solution)/shard_map/all_to_all | solution.py:230
  60.6 2.7 %attend.1.attn = bf16[256,384]{1,0:T(8,128)(2,1)S(1)} custom-call(s32[16]{0:T(128)S(1)} %and_select_fusion.lookup, bf16[8,32,384]{2,1,0:T(8,128)(2,1)S(1)} %copy-done.6, bf16[8,32,384]{2,1,0:T(8,128)(2,1)S(1)} %copy-done.1, bf16[8,32,384]{2,1,0:T(8,128)(2,1)S(1)} %copy-done.3, bf16[16,2,32,384]{3,2,1,0:T(8,128)(2,1)S(1)} %all-to-all-done.got), custom_call_target="tpu_custom_call" | custom-call | flops 2000000000 | bytes 8000000 | tf_op jit(solution)/shard_map/attend/pallas_call | solution.py:243
  63.4 1.3 %send.1 = bf16[8,192,384]{2,1,0:T(8,128)(2,1)S(1)} custom-call(s32[1]{0:T(128)} %bitcast.5.side, bf16[8,256,384]{2,1,0:T(8,128)(2,1)S(1)} %copy-done.5, bf16[256,384]{1,0:T(8,128)(2,1)S(1)} %attend.1.attn), custom_call_target="tpu_custom_call" | custom-call | flops 3000000000 | bytes 3000000 | tf_op jit(solution)/shard_map/send/pallas_call | solution.py:256
  64.7 1.9 %collective-permute-start.4 = (bf16[8,192,384]{2,1,0:T(8,128)(2,1)S(1)}, bf16[8,192,384]{2,1,0:T(8,128)(2,1)S(1)}, u32[]{:S(2)}, u32[]{:S(2)}) collective-permute-start(bf16[8,192,384]{2,1,0:T(8,128)(2,1)S(1)} %send.1), channel_id=1, source_target_pairs={{0,8},{8,0},{1,9},{9,1},{2,10},{10,2},{3,11},{11,3},{4,12},{12,4},... | collective-permute-start | bytes 3538952 | tf_op jit(solution)/shard_map/ppermute | solution.py:267
  66.7 2.4 %collective-permute-start.3 = (bf16[3,8,48,384]{3,2,1,0:T(8,128)(2,1)S(1)}, bf16[3,8,48,384]{3,2,1,0:T(8,128)(2,1)}, u32[]{:S(2)}, u32[]{:S(2)}) collective-permute-start(bf16[3,8,48,384]{3,2,1,0:T(8,128)(2,1)S(1)} %join.1.halves), channel_id=1, source_target_pairs={{0,8},{8,0},{1,9},{9,1},{2,10},{10,2},{3,11},{11,3},{4,12},{12,4},... | collective-permute-start | bytes 2654216 | tf_op jit(solution)/shard_map/ppermute | solution.py:287
  69.1 1.3 %keep.1.ours = bf16[8,192,384]{2,1,0:T(8,128)(2,1)S(1)} custom-call(s32[1]{0:T(128)} %bitcast.1.side, bf16[8,256,384]{2,1,0:T(8,128)(2,1)S(1)} %copy-done.5, bf16[256,384]{1,0:T(8,128)(2,1)S(1)} %attend.1.attn), custom_call_target="tpu_custom_call" | custom-call | flops 3000000000 | bytes 3000000 | tf_op jit(solution)/shard_map/keep/pallas_call | solution.py:256
  70.5 1.1 add.36
  71.8 0.8 copy-done.2
  72.6 0.1 copy-done.7
  72.7 0.1 copy-done.9
  72.8 7.7 %backward.1 = (bf16[8,32,384]{2,1,0:T(8,128)(2,1)}, bf16[16,2,32,384]{3,2,1,0:T(8,128)(2,1)S(1)}, f32[256,384]{1,0:T(8,128)S(1)}, f32[256,384]{1,0:T(8,128)S(1)}) custom-call(s32[16]{0:T(128)S(1)} %and_select_fusion.lookup, s32[2]{0:T(128)S(1)} %pad_add_fusion.place, bf16[8,32,384]{2,1,0:T(8,128)(2,1)S(1)} %copy-done.7, bf16[8,32,384]{2,1,0:T(8,128)(2,1)S(1)} %copy-done.2, ...), custom_call_target="tpu_custom_call" | custom-call | flops 6000000000 | bytes 9000000 | tf_op jit(solution)/shard_map/backward/pallas_call | solution.py:290
  80.5 34.0 %all_to_all.10.came = bf16[16,2,32,384]{3,2,1,0:T(8,128)(2,1)S(1)} all-to-all(bf16[16,2,32,384]{3,2,1,0:T(8,128)(2,1)S(1)} %get-tuple-element.35), channel_id=1, replica_groups=mesh['dp'=4,'y'=8,'core'=2,'head'=8] {'y','core'}, dimensions={0} | all-to-all | bytes 1572864 | tf_op jit(solution)/shard_map/all_to_all | solution.py:321
  114.5 1.5 %finish.1 = (bf16[8,32,384]{2,1,0:T(8,128)(2,1)}, bf16[8,32,384]{2,1,0:T(8,128)(2,1)}) custom-call(s32[16]{0:T(128)S(1)} %fusion.4.source, bf16[16,2,32,384]{3,2,1,0:T(8,128)(2,1)S(1)} %all_to_all.10.came, f32[256,384]{1,0:T(8,128)S(1)} %get-tuple-element.36.own_dk, f32[256,384]{1,0:T(8,128)S(1)} %get-tuple-element.37.own_dv), custom_call_target="tpu_custom_call" | custom-call | flops 1000000 | bytes 3000000 | tf_op jit(solution)/shard_map/finish/pallas_call | solution.py:323
  116.0 2.5 %reduce-scatter.2.cloned.1.call-done = bf16[1,192,384]{2,1,0:T(8,128)(2,1)} async-done(((bf16[8,192,384]{2,1,0:T(8,128)(2,1)}), bf16[1,192,384]{2,1,0:T(8,128)(2,1)}) %reduce-scatter.2.cloned.1.call-update) | async-done | bytes 147472 | tf_op jit(solution)/shard_map/reduce_scatter | solution.py:288
  118.6 1.6 %bitcast_convert_fusion = f32[192,384]{1,0:T(8,128)} fusion(bf16[1,192,384]{2,1,0:T(8,128)(2,1)} %reduce-scatter.2.cloned.1.call-done), kind=kLoop, calls=%fused_computation | loop fusion | flops 73728 | bytes 442368 | tf_op jit(solution)/shard_map/convert_element_type | solution.py:333
  (37 shorter events, 0.7 us)
Async XLA Ops:
  7.2 1.6 %copy-start = (bf16[192,384]{1,0:T(8,128)(2,1)S(1)}, bf16[192,384]{1,0:T(8,128)(2,1)}, u32[]{:S(2)}) copy-start(bf16[192,384]{1,0:T(8,128)(2,1)} %param.12) | copy-start | bytes 442372
  7.2 25.3 %copy-start.1 = (bf16[8,32,384]{2,1,0:T(8,128)(2,1)S(1)}, bf16[8,32,384]{2,1,0:T(8,128)(2,1)}, u32[]{:S(2)}) copy-start(bf16[8,32,384]{2,1,0:T(8,128)(2,1)} %keys.5) | copy-start | bytes 589828
  7.2 25.3 %copy-start.3 = (bf16[8,32,384]{2,1,0:T(8,128)(2,1)S(1)}, bf16[8,32,384]{2,1,0:T(8,128)(2,1)}, u32[]{:S(2)}) copy-start(bf16[8,32,384]{2,1,0:T(8,128)(2,1)} %values.5) | copy-start | bytes 589828
  7.2 53.4 %all-gather.3.cloned.1.call-start = ((), (), s32[]{:S(2)}) async-start(), calls=%async_computation.3 | async-start | bytes 1769472 | tf_op jit(solution)/shard_map/all_gather | solution.py:211
  34.2 12.9 %copy-start.10 = (s32[2,8]{1,0:T(2,128)S(1)}, s32[2,8]{1,0:T(2,128)}, u32[]{:S(2)}) copy-start(s32[2,8]{1,0:T(2,128)} %param.13) | copy-start | bytes 196
  34.2 26.4 %copy-start.6 = (bf16[8,32,384]{2,1,0:T(8,128)(2,1)S(1)}, bf16[8,32,384]{2,1,0:T(8,128)(2,1)}, u32[]{:S(2)}) copy-start(bf16[8,32,384]{2,1,0:T(8,128)(2,1)} %queries.3) | copy-start | bytes 589828
  34.2 26.4 %all-to-all-start = ((bf16[16,2,32,384]{3,2,1,0:T(8,128)(2,1)}), bf16[16,2,32,384]{3,2,1,0:T(8,128)(2,1)S(1)}, u32[]{:S(2)}, u32[]{:S(2)}) async-start(bf16[16,2,32,384]{3,2,1,0:T(8,128)(2,1)} %pack.1), calls=%async_computation | async-start | bytes 1572864 | tf_op jit(solution)/shard_map/all_to_all | solution.py:230
  37.9 80.7 %reduce-scatter.2.cloned.1.call-start = ((), (), s32[]{:S(2)}) async-start(), calls=%async_computation.4 | async-start | bytes 1327104 | tf_op jit(solution)/shard_map/reduce_scatter | solution.py:288
  38.0 25.4 %collective-permute-start = (bf16[8,48,384]{2,1,0:T(8,128)(2,1)S(1)}, bf16[8,48,384]{2,1,0:T(8,128)(2,1)S(1)}, u32[]{:S(2)}, u32[]{:S(2)}) collective-permute-start(bf16[8,48,384]{2,1,0:T(8,128)(2,1)S(1)} %constant_dynamic-slice_fusion), channel_id=1, source_target_pairs={{0,128},{128,256},{256,384},{384,0},{1,129},{129,257},{257,385},{3... | collective-permute-start | bytes 884744 | tf_op jit(solution)/shard_map/ppermute | solution.py:234
  39.9 23.4 %collective-permute-start.1 = (bf16[8,48,384]{2,1,0:T(8,128)(2,1)S(1)}, bf16[8,48,384]{2,1,0:T(8,128)(2,1)S(1)}, u32[]{:S(2)}, u32[]{:S(2)}) collective-permute-start(bf16[8,48,384]{2,1,0:T(8,128)(2,1)S(1)} %constant_dynamic-slice_fusion), channel_id=1, source_target_pairs={{0,256},{128,384},{256,0},{384,128},{1,257},{129,385},{257,1},{385... | collective-permute-start | bytes 884744 | tf_op jit(solution)/shard_map/ppermute | solution.py:234
  44.0 19.4 %collective-permute-start.2 = (bf16[8,48,384]{2,1,0:T(8,128)(2,1)S(1)}, bf16[8,48,384]{2,1,0:T(8,128)(2,1)S(1)}, u32[]{:S(2)}, u32[]{:S(2)}) collective-permute-start(bf16[8,48,384]{2,1,0:T(8,128)(2,1)S(1)} %constant_dynamic-slice_fusion), channel_id=1, source_target_pairs={{0,384},{128,0},{256,128},{384,256},{1,385},{129,1},{257,129},{385... | collective-permute-start | bytes 884744 | tf_op jit(solution)/shard_map/ppermute | solution.py:234
  60.6 2.8 %copy-start.5 = (bf16[8,256,384]{2,1,0:T(8,128)(2,1)S(1)}, bf16[8,256,384]{2,1,0:T(8,128)(2,1)}, u32[]{:S(2)}) copy-start(bf16[8,256,384]{2,1,0:T(8,128)(2,1)} %all-gather.3.cloned.1.call-done.grad_far.grad) | copy-start | bytes 4718596
  63.3 5.8 %copy-start.8 = (bf16[256,384]{1,0:T(8,128)(2,1)}, bf16[256,384]{1,0:T(8,128)(2,1)S(1)}, u32[]{:S(2)}) copy-start(bf16[256,384]{1,0:T(8,128)(2,1)S(1)} %attend.1.attn) | copy-start | bytes 589828
  64.7 5.8 %collective-permute-start.4 = (bf16[8,192,384]{2,1,0:T(8,128)(2,1)S(1)}, bf16[8,192,384]{2,1,0:T(8,128)(2,1)S(1)}, u32[]{:S(2)}, u32[]{:S(2)}) collective-permute-start(bf16[8,192,384]{2,1,0:T(8,128)(2,1)S(1)} %send.1), channel_id=1, source_target_pairs={{0,8},{8,0},{1,9},{9,1},{2,10},{10,2},{3,11},{11,3},{4,12},{12,4},... | collective-permute-start | bytes 3538952 | tf_op jit(solution)/shard_map/ppermute | solution.py:267
  66.7 5.0 %collective-permute-start.3 = (bf16[3,8,48,384]{3,2,1,0:T(8,128)(2,1)S(1)}, bf16[3,8,48,384]{3,2,1,0:T(8,128)(2,1)}, u32[]{:S(2)}, u32[]{:S(2)}) collective-permute-start(bf16[3,8,48,384]{3,2,1,0:T(8,128)(2,1)S(1)} %join.1.halves), channel_id=1, source_target_pairs={{0,8},{8,0},{1,9},{9,1},{2,10},{10,2},{3,11},{11,3},{4,12},{12,4},... | collective-permute-start | bytes 2654216 | tf_op jit(solution)/shard_map/ppermute | solution.py:287
  71.6 0.9 copy-start.2
  71.6 1.0 copy-start.4
  71.6 1.1 copy-start.7
  71.6 1.2 copy-start.9
Sparse Core Ops, SparseCore 0:
  10.1 45.0 all-gather.2
  71.8 46.7 reduce-scatter.1

commit v5 on v4

--- a/solution.py
+++ b/solution.py
@@ -10,7 +10,7 @@
 HD = 128
 CF = 4
 RET = 8
-LIST_ROWS = 16
+LIST_ROWS = 8
 BF = jnp.bfloat16
 F32 = jnp.float32
 HBM = pl.BlockSpec(memory_space=pltpu.HBM)
@@ -37,18 +37,11 @@
     return pl.CostEstimate(flops=flops, bytes_accessed=nbytes, transcendentals=0)
 
 
-def pack_body(source, keys, values, out, sems):
-    copies = []
+def pack_body(source, keys, values, out):
     for shard in range(out.shape[0]):
         frame = source[shard]
-        for which, held in enumerate((keys, values)):
-            copy = pltpu.make_async_copy(
-                held.at[frame], out.at[shard, which], sems.at[shard, which]
-            )
-            copy.start()
-            copies.append(copy)
-    for copy in copies:
-        copy.wait()
+        out[shard, 0] = keys[frame]
+        out[shard, 1] = values[frame]
 
 
 def fill_sets(lookup, group, keys, values, got, key_set, value_set):
@@ -221,8 +214,7 @@
         pack_body,
         out_shape=shape((shards, 2, tokens, width), BF),
         in_specs=[SMEM, VMEM, VMEM],
-        out_specs=HBM,
-        scratch_shapes=[dma((shards, 2))],
+        out_specs=VMEM,
         compiler_params=params(),
         cost_estimate=cost(0, 4 * shards * tokens * width * 2),
         name="pack",

time: 129 us -> 129 us (level)
  the two profiles are of different devices: /device:TPU:1 before, /device:TPU:2 now
where the time goes in v5:
time: 129 us; the launch traced here: 128 us
  blocking collectives  54.4 us (42%)
  starting transfers between devices  19.4 us (15%)
  waiting for transfers between devices  19.1 us (15%)
  Pallas kernels  17.2 us (13%)
  between operations  14.3 us (11%)
  other arithmetic  2.56 us (2%)
  local copies, waits for them, and re-layouts  1.34 us (1%)
    all_to_all x1, blocking collectives, per_device(): came = lax.all_to_all(back, time, split_axis=0, concat_axis=0, tiled=True)  34.9 us
    all_gather x1, blocking collectives, per_device(): lax.all_gather(jnp.concatenate([part, names], axis=0), time, axis=0, tile...  19.5 us
    ppermute x3, starting transfers between devices, per_device(): lax.ppermute(mine, 'dp', [(i, (i + s) % parts) for i in range(parts)])  10.5 us
    all_to_all x1, waiting for transfers between devices, per_device(): got = lax.all_to_all(packed, time, split_axis=0, concat_axis=0, tiled=True)  9.98 us
    pallas_call x1, Pallas kernels, per_device(): pl.pallas_call(functools.partial(backward_body, parts), out_shape=(shape(...  7.68 us
    reduce_scatter x1, waiting for transfers between devices, per_device(): lax.psum_scatter(chip_sum, 'y', scatter_dimension=0, tiled=False)  5.27 us
    all_to_all x1, starting transfers between devices, per_device(): got = lax.all_to_all(packed, time, split_axis=0, concat_axis=0, tiled=True)  4.55 us
    all_gather x1, waiting for transfers between devices, per_device(): lax.all_gather(out_grad.reshape(rows, width), 'head', axis=0, tiled=False)  3.15 us
  transfers between devices with their start and end apart: 8, of which 3 were waited for; matrix products, arithmetic and copies ran while one was open for 1% of the time, Pallas kernels for 12%

profile of v5, /device:TPU:2, one launch (start us, length us, event | category | flops | bytes accessed | tf_op | source)
XLA Modules:
  0.0 128.3 jit_solution(14513946727484743268)
XLA Ops:
  7.2 0.7 all-gather.3.cloned.1.call-update
  7.9 0.7 convert_element_type.23
  8.7 19.5 %all-gather = bf16[896,384]{1,0:T(8,128)(2,1)S(1)} all-gather(bf16[56,384]{1,0:T(8,128)(2,1)S(1)} %fusion.1), channel_id=2, replica_groups=mesh['dp'=4,'y'=8,'core'=2,'head'=8] {'y','core'}, dimensions={0}, use_global_device_ids=true | all-gather | bytes 731136 | tf_op jit(solution)/shard_map/all_gather | solution.py:208
  28.2 0.1 fusion.4.source
  28.4 1.5 %pack.1 = bf16[16,2,32,384]{3,2,1,0:T(8,128)(2,1)} custom-call(s32[16]{0:T(128)S(1)} %fusion.4.source, bf16[8,32,384]{2,1,0:T(8,128)(2,1)S(1)} %copy-done.1, bf16[8,32,384]{2,1,0:T(8,128)(2,1)S(1)} %copy-done.3), custom_call_target="tpu_custom_call" | custom-call | bytes 1572864 | tf_op jit(solution)/shard_map/pack/pallas_call | solution.py:213
  29.9 4.5 %all-to-all-start = ((bf16[16,2,32,384]{3,2,1,0:T(8,128)(2,1)}), bf16[16,2,32,384]{3,2,1,0:T(8,128)(2,1)S(1)}, u32[]{:S(2)}, u32[]{:S(2)}) async-start(bf16[16,2,32,384]{3,2,1,0:T(8,128)(2,1)} %pack.1), calls=%async_computation | async-start | bytes 1572864 | tf_op jit(solution)/shard_map/all_to_all | solution.py:222
  34.5 3.4 %collective-permute-start = (bf16[8,48,384]{2,1,0:T(8,128)(2,1)S(1)}, bf16[8,48,384]{2,1,0:T(8,128)(2,1)S(1)}, u32[]{:S(2)}, u32[]{:S(2)}) collective-permute-start(bf16[8,48,384]{2,1,0:T(8,128)(2,1)S(1)} %constant_dynamic-slice_fusion), channel_id=1, source_target_pairs={{0,128},{128,256},{256,384},{384,0},{1,129},{129,257},{257,385},{3... | collective-permute-start | bytes 884744 | tf_op jit(solution)/shard_map/ppermute | solution.py:226
  37.9 4.6 %collective-permute-start.1 = (bf16[8,48,384]{2,1,0:T(8,128)(2,1)S(1)}, bf16[8,48,384]{2,1,0:T(8,128)(2,1)S(1)}, u32[]{:S(2)}, u32[]{:S(2)}) collective-permute-start(bf16[8,48,384]{2,1,0:T(8,128)(2,1)S(1)} %constant_dynamic-slice_fusion), channel_id=1, source_target_pairs={{0,256},{128,384},{256,0},{384,128},{1,257},{129,385},{257,1},{385... | collective-permute-start | bytes 884744 | tf_op jit(solution)/shard_map/ppermute | solution.py:226
  42.5 2.5 %collective-permute-start.2 = (bf16[8,48,384]{2,1,0:T(8,128)(2,1)S(1)}, bf16[8,48,384]{2,1,0:T(8,128)(2,1)S(1)}, u32[]{:S(2)}, u32[]{:S(2)}) collective-permute-start(bf16[8,48,384]{2,1,0:T(8,128)(2,1)S(1)} %constant_dynamic-slice_fusion), channel_id=1, source_target_pairs={{0,384},{128,0},{256,128},{384,256},{1,385},{129,1},{257,129},{385... | collective-permute-start | bytes 884744 | tf_op jit(solution)/shard_map/ppermute | solution.py:226
  45.1 10.0 %all-to-all-done.got = bf16[16,2,32,384]{3,2,1,0:T(8,128)(2,1)S(1)} async-done(((bf16[16,2,32,384]{3,2,1,0:T(8,128)(2,1)}), bf16[16,2,32,384]{3,2,1,0:T(8,128)(2,1)S(1)}, u32[]{:S(2)}, u32[]{:S(2)}) %all-to-all-start) | async-done | bytes 786464 | tf_op jit(solution)/shard_map/all_to_all | solution.py:222
  55.1 3.1 %all-gather.3.cloned.1.call-done.grad_far.grad = bf16[8,256,384]{2,1,0:T(8,128)(2,1)} async-done(((bf16[1,256,384]{2,1,0:T(8,128)(2,1)}), bf16[8,256,384]{2,1,0:T(8,128)(2,1)}) %all-gather.3.cloned.1.call-update) | async-done | bytes 1572880 | tf_op jit(solution)/shard_map/all_gather | solution.py:204
  58.3 2.7 %attend.1.attn = bf16[256,384]{1,0:T(8,128)(2,1)S(1)} custom-call(s32[16]{0:T(128)S(1)} %and_select_fusion.lookup, bf16[8,32,384]{2,1,0:T(8,128)(2,1)S(1)} %copy-done.6, bf16[8,32,384]{2,1,0:T(8,128)(2,1)S(1)} %copy-done.1, bf16[8,32,384]{2,1,0:T(8,128)(2,1)S(1)} %copy-done.3, bf16[16,2,32,384]{3,2,1,0:T(8,128)(2,1)S(1)} %all-to-all-done.got), custom_call_target="tpu_custom_call" | custom-call | flops 2000000000 | bytes 8000000 | tf_op jit(solution)/shard_map/attend/pallas_call | solution.py:235
  61.0 1.3 %send.1 = bf16[8,192,384]{2,1,0:T(8,128)(2,1)S(1)} custom-call(s32[1]{0:T(128)} %bitcast.5.side, bf16[8,256,384]{2,1,0:T(8,128)(2,1)S(1)} %copy-done.5, bf16[256,384]{1,0:T(8,128)(2,1)S(1)} %attend.1.attn), custom_call_target="tpu_custom_call" | custom-call | flops 3000000000 | bytes 3000000 | tf_op jit(solution)/shard_map/send/pallas_call | solution.py:248
  62.4 1.9 %collective-permute-start.4 = (bf16[8,192,384]{2,1,0:T(8,128)(2,1)S(1)}, bf16[8,192,384]{2,1,0:T(8,128)(2,1)S(1)}, u32[]{:S(2)}, u32[]{:S(2)}) collective-permute-start(bf16[8,192,384]{2,1,0:T(8,128)(2,1)S(1)} %send.1), channel_id=1, source_target_pairs={{0,8},{8,0},{1,9},{9,1},{2,10},{10,2},{3,11},{11,3},{4,12},{12,4},... | collective-permute-start | bytes 3538952 | tf_op jit(solution)/shard_map/ppermute | solution.py:259
  64.4 2.4 %collective-permute-start.3 = (bf16[3,8,48,384]{3,2,1,0:T(8,128)(2,1)S(1)}, bf16[3,8,48,384]{3,2,1,0:T(8,128)(2,1)}, u32[]{:S(2)}, u32[]{:S(2)}) collective-permute-start(bf16[3,8,48,384]{3,2,1,0:T(8,128)(2,1)S(1)} %join.1.halves), channel_id=1, source_target_pairs={{0,8},{8,0},{1,9},{9,1},{2,10},{10,2},{3,11},{11,3},{4,12},{12,4},... | collective-permute-start | bytes 2654216 | tf_op jit(solution)/shard_map/ppermute | solution.py:279
  66.8 1.3 %keep.1.ours = bf16[8,192,384]{2,1,0:T(8,128)(2,1)S(1)} custom-call(s32[1]{0:T(128)} %bitcast.1.side, bf16[8,256,384]{2,1,0:T(8,128)(2,1)S(1)} %copy-done.5, bf16[256,384]{1,0:T(8,128)(2,1)S(1)} %attend.1.attn), custom_call_target="tpu_custom_call" | custom-call | flops 3000000000 | bytes 3000000 | tf_op jit(solution)/shard_map/keep/pallas_call | solution.py:248
  68.1 1.1 add.36
  69.4 0.8 copy-done.2
  70.4 0.1 copy-done.9
  70.5 7.7 %backward.1 = (bf16[8,32,384]{2,1,0:T(8,128)(2,1)}, bf16[16,2,32,384]{3,2,1,0:T(8,128)(2,1)S(1)}, f32[256,384]{1,0:T(8,128)S(1)}, f32[256,384]{1,0:T(8,128)S(1)}) custom-call(s32[16]{0:T(128)S(1)} %and_select_fusion.lookup, s32[2]{0:T(128)S(1)} %pad_add_fusion.place, bf16[8,32,384]{2,1,0:T(8,128)(2,1)S(1)} %copy-done.7, bf16[8,32,384]{2,1,0:T(8,128)(2,1)S(1)} %copy-done.2, ...), custom_call_target="tpu_custom_call" | custom-call | flops 6000000000 | bytes 9000000 | tf_op jit(solution)/shard_map/backward/pallas_call | solution.py:282
  78.2 34.9 %all_to_all.10.came = bf16[16,2,32,384]{3,2,1,0:T(8,128)(2,1)S(1)} all-to-all(bf16[16,2,32,384]{3,2,1,0:T(8,128)(2,1)S(1)} %get-tuple-element.35), channel_id=1, replica_groups=mesh['dp'=4,'y'=8,'core'=2,'head'=8] {'y','core'}, dimensions={0} | all-to-all | bytes 1572864 | tf_op jit(solution)/shard_map/all_to_all | solution.py:313
  113.1 1.5 %finish.1 = (bf16[8,32,384]{2,1,0:T(8,128)(2,1)}, bf16[8,32,384]{2,1,0:T(8,128)(2,1)}) custom-call(s32[16]{0:T(128)S(1)} %fusion.4.source, bf16[16,2,32,384]{3,2,1,0:T(8,128)(2,1)S(1)} %all_to_all.10.came, f32[256,384]{1,0:T(8,128)S(1)} %get-tuple-element.36.own_dk, f32[256,384]{1,0:T(8,128)S(1)} %get-tuple-element.37.own_dv), custom_call_target="tpu_custom_call" | custom-call | flops 1000000 | bytes 3000000 | tf_op jit(solution)/shard_map/finish/pallas_call | solution.py:315
  114.6 5.3 %reduce-scatter.2.cloned.1.call-done = bf16[1,192,384]{2,1,0:T(8,128)(2,1)} async-done(((bf16[8,192,384]{2,1,0:T(8,128)(2,1)}), bf16[1,192,384]{2,1,0:T(8,128)(2,1)}) %reduce-scatter.2.cloned.1.call-update) | async-done | bytes 147472 | tf_op jit(solution)/shard_map/reduce_scatter | solution.py:280
  119.9 1.6 %bitcast_convert_fusion = f32[192,384]{1,0:T(8,128)} fusion(bf16[1,192,384]{2,1,0:T(8,128)(2,1)} %reduce-scatter.2.cloned.1.call-done), kind=kLoop, calls=%fused_computation | loop fusion | flops 73728 | bytes 442368 | tf_op jit(solution)/shard_map/convert_element_type | solution.py:325
  (37 shorter events, 0.8 us)
Async XLA Ops:
  7.2 1.6 %copy-start = (bf16[192,384]{1,0:T(8,128)(2,1)S(1)}, bf16[192,384]{1,0:T(8,128)(2,1)}, u32[]{:S(2)}) copy-start(bf16[192,384]{1,0:T(8,128)(2,1)} %param.12) | copy-start | bytes 442372
  7.2 21.2 %copy-start.1 = (bf16[8,32,384]{2,1,0:T(8,128)(2,1)S(1)}, bf16[8,32,384]{2,1,0:T(8,128)(2,1)}, u32[]{:S(2)}) copy-start(bf16[8,32,384]{2,1,0:T(8,128)(2,1)} %keys.5) | copy-start | bytes 589828
  7.2 21.2 %copy-start.3 = (bf16[8,32,384]{2,1,0:T(8,128)(2,1)S(1)}, bf16[8,32,384]{2,1,0:T(8,128)(2,1)}, u32[]{:S(2)}) copy-start(bf16[8,32,384]{2,1,0:T(8,128)(2,1)} %values.5) | copy-start | bytes 589828
  7.2 51.0 %all-gather.3.cloned.1.call-start = ((), (), s32[]{:S(2)}) async-start(), calls=%async_computation.3 | async-start | bytes 1769472 | tf_op jit(solution)/shard_map/all_gather | solution.py:204
  29.9 15.2 %copy-start.10 = (s32[2,8]{1,0:T(2,128)S(1)}, s32[2,8]{1,0:T(2,128)}, u32[]{:S(2)}) copy-start(s32[2,8]{1,0:T(2,128)} %param.13) | copy-start | bytes 196
  29.9 28.4 %copy-start.6 = (bf16[8,32,384]{2,1,0:T(8,128)(2,1)S(1)}, bf16[8,32,384]{2,1,0:T(8,128)(2,1)}, u32[]{:S(2)}) copy-start(bf16[8,32,384]{2,1,0:T(8,128)(2,1)} %queries.3) | copy-start | bytes 589828
  29.9 25.2 %all-to-all-start = ((bf16[16,2,32,384]{3,2,1,0:T(8,128)(2,1)}), bf16[16,2,32,384]{3,2,1,0:T(8,128)(2,1)S(1)}, u32[]{:S(2)}, u32[]{:S(2)}) async-start(bf16[16,2,32,384]{3,2,1,0:T(8,128)(2,1)} %pack.1), calls=%async_computation | async-start | bytes 1572864 | tf_op jit(solution)/shard_map/all_to_all | solution.py:222
  34.4 85.4 %reduce-scatter.2.cloned.1.call-start = ((), (), s32[]{:S(2)}) async-start(), calls=%async_computation.4 | async-start | bytes 1327104 | tf_op jit(solution)/shard_map/reduce_scatter | solution.py:280
  34.5 26.5 %collective-permute-start = (bf16[8,48,384]{2,1,0:T(8,128)(2,1)S(1)}, bf16[8,48,384]{2,1,0:T(8,128)(2,1)S(1)}, u32[]{:S(2)}, u32[]{:S(2)}) collective-permute-start(bf16[8,48,384]{2,1,0:T(8,128)(2,1)S(1)} %constant_dynamic-slice_fusion), channel_id=1, source_target_pairs={{0,128},{128,256},{256,384},{384,0},{1,129},{129,257},{257,385},{3... | collective-permute-start | bytes 884744 | tf_op jit(solution)/shard_map/ppermute | solution.py:226
  37.9 23.1 %collective-permute-start.1 = (bf16[8,48,384]{2,1,0:T(8,128)(2,1)S(1)}, bf16[8,48,384]{2,1,0:T(8,128)(2,1)S(1)}, u32[]{:S(2)}, u32[]{:S(2)}) collective-permute-start(bf16[8,48,384]{2,1,0:T(8,128)(2,1)S(1)} %constant_dynamic-slice_fusion), channel_id=1, source_target_pairs={{0,256},{128,384},{256,0},{384,128},{1,257},{129,385},{257,1},{385... | collective-permute-start | bytes 884744 | tf_op jit(solution)/shard_map/ppermute | solution.py:226
  42.5 18.5 %collective-permute-start.2 = (bf16[8,48,384]{2,1,0:T(8,128)(2,1)S(1)}, bf16[8,48,384]{2,1,0:T(8,128)(2,1)S(1)}, u32[]{:S(2)}, u32[]{:S(2)}) collective-permute-start(bf16[8,48,384]{2,1,0:T(8,128)(2,1)S(1)} %constant_dynamic-slice_fusion), channel_id=1, source_target_pairs={{0,384},{128,0},{256,128},{384,256},{1,385},{129,1},{257,129},{385... | collective-permute-start | bytes 884744 | tf_op jit(solution)/shard_map/ppermute | solution.py:226
  58.3 2.8 %copy-start.5 = (bf16[8,256,384]{2,1,0:T(8,128)(2,1)S(1)}, bf16[8,256,384]{2,1,0:T(8,128)(2,1)}, u32[]{:S(2)}) copy-start(bf16[8,256,384]{2,1,0:T(8,128)(2,1)} %all-gather.3.cloned.1.call-done.grad_far.grad) | copy-start | bytes 4718596
  61.0 5.8 %copy-start.8 = (bf16[256,384]{1,0:T(8,128)(2,1)}, bf16[256,384]{1,0:T(8,128)(2,1)S(1)}, u32[]{:S(2)}) copy-start(bf16[256,384]{1,0:T(8,128)(2,1)S(1)} %attend.1.attn) | copy-start | bytes 589828
  62.4 5.8 %collective-permute-start.4 = (bf16[8,192,384]{2,1,0:T(8,128)(2,1)S(1)}, bf16[8,192,384]{2,1,0:T(8,128)(2,1)S(1)}, u32[]{:S(2)}, u32[]{:S(2)}) collective-permute-start(bf16[8,192,384]{2,1,0:T(8,128)(2,1)S(1)} %send.1), channel_id=1, source_target_pairs={{0,8},{8,0},{1,9},{9,1},{2,10},{10,2},{3,11},{11,3},{4,12},{12,4},... | collective-permute-start | bytes 3538952 | tf_op jit(solution)/shard_map/ppermute | solution.py:259
  64.4 5.0 %collective-permute-start.3 = (bf16[3,8,48,384]{3,2,1,0:T(8,128)(2,1)S(1)}, bf16[3,8,48,384]{3,2,1,0:T(8,128)(2,1)}, u32[]{:S(2)}, u32[]{:S(2)}) collective-permute-start(bf16[3,8,48,384]{3,2,1,0:T(8,128)(2,1)S(1)} %join.1.halves), channel_id=1, source_target_pairs={{0,8},{8,0},{1,9},{9,1},{2,10},{10,2},{3,11},{11,3},{4,12},{12,4},... | collective-permute-start | bytes 2654216 | tf_op jit(solution)/shard_map/ppermute | solution.py:279
  69.3 0.9 copy-start.2
  69.3 1.0 copy-start.4
  69.3 1.1 copy-start.7
  69.3 1.2 copy-start.9
Sparse Core Ops, SparseCore 0:
  10.1 48.0 all-gather.2
  69.4 50.3 reduce-scatter.1

commit v6 on v5

--- a/solution.py
+++ b/solution.py
@@ -37,11 +37,13 @@
     return pl.CostEstimate(flops=flops, bytes_accessed=nbytes, transcendentals=0)
 
 
-def pack_body(source, keys, values, out):
+def pack_body(source, keys, values, out, own_keys, own_values):
     for shard in range(out.shape[0]):
         frame = source[shard]
         out[shard, 0] = keys[frame]
         out[shard, 1] = values[frame]
+    own_keys[...] = keys[...]
+    own_values[...] = values[...]
 
 
 def fill_sets(lookup, group, keys, values, got, key_set, value_set):
@@ -210,11 +212,12 @@
     source = jnp.max(jnp.where(wanted // frames == myself, wanted % frames, 0), axis=1)
     lookup = lists.reshape(entries) // frames
 
-    packed = pl.pallas_call(
+    packed, keys, values = pl.pallas_call(
         pack_body,
-        out_shape=shape((shards, 2, tokens, width), BF),
+        out_shape=(shape((shards, 2, tokens, width), BF),)
+        + (shape((frames, tokens, width), BF),) * 2,
         in_specs=[SMEM, VMEM, VMEM],
-        out_specs=VMEM,
+        out_specs=(VMEM,) * 3,
         compiler_params=params(),
         cost_estimate=cost(0, 4 * shards * tokens * width * 2),
         name="pack",

time: 129 us -> 130 us (level)
  the two profiles are of different devices: /device:TPU:2 before, /device:TPU:1 now
where the time goes in v6:
time: 130 us; the launch traced here: 127 us
  blocking collectives  57.5 us (44%)
  starting transfers between devices  17.2 us (13%)
  Pallas kernels  16.7 us (13%)
  waiting for transfers between devices  14.4 us (11%)
  between operations  14.3 us (11%)
  local copies, waits for them, and re-layouts  4.67 us (4%)
  other arithmetic  2.56 us (2%)
    all_to_all x1, blocking collectives, per_device(): came = lax.all_to_all(back, time, split_axis=0, concat_axis=0, tiled=True)  34.3 us
    all_gather x1, blocking collectives, per_device(): lax.all_gather(jnp.concatenate([part, names], axis=0), time, axis=0, tile...  23.2 us
    all_to_all x1, waiting for transfers between devices, per_device(): got = lax.all_to_all(packed, time, split_axis=0, concat_axis=0, tiled=True)  12.6 us
    ppermute x3, starting transfers between devices, per_device(): lax.ppermute(mine, 'dp', [(i, (i + s) % parts) for i in range(parts)])  9.13 us
    pallas_call x1, Pallas kernels, per_device(): pl.pallas_call(functools.partial(backward_body, parts), out_shape=(shape(...  7.1 us
    unnamed x26, local copies, waits for them, and re-layouts  3.75 us
    all_to_all x1, starting transfers between devices, per_device(): got = lax.all_to_all(packed, time, split_axis=0, concat_axis=0, tiled=True)  3.71 us
    pallas_call x1, Pallas kernels, per_device(): pl.pallas_call(attend_body, out_shape=shape((rows, width), BF), in_specs=...  2.73 us
  transfers between devices with their start and end apart: 8, of which 2 were waited for; matrix products, arithmetic and copies ran while one was open for 1% of the time, Pallas kernels for 12%

profile of v6, /device:TPU:1, one launch (start us, length us, event | category | flops | bytes accessed | tf_op | source)
XLA Modules:
  0.0 127.3 jit_solution(14754020717199250323)
XLA Ops:
  7.9 0.7 convert_element_type.23
  8.7 23.2 %all-gather = bf16[896,384]{1,0:T(8,128)(2,1)S(1)} all-gather(bf16[56,384]{1,0:T(8,128)(2,1)S(1)} %fusion.1), channel_id=2, replica_groups=mesh['dp'=4,'y'=8,'core'=2,'head'=8] {'y','core'}, dimensions={0}, use_global_device_ids=true | all-gather | bytes 731136 | tf_op jit(solution)/shard_map/all_gather | solution.py:210
  32.0 1.5 %pack.1 = (bf16[16,2,32,384]{3,2,1,0:T(8,128)(2,1)}, bf16[8,32,384]{2,1,0:T(8,128)(2,1)S(1)}, bf16[8,32,384]{2,1,0:T(8,128)(2,1)S(1)}) custom-call(s32[16]{0:T(128)S(1)} %fusion.4.source, bf16[8,32,384]{2,1,0:T(8,128)(2,1)S(1)} %copy-done.1, bf16[8,32,384]{2,1,0:T(8,128)(2,1)S(1)} %copy-done.2), custom_call_target="tpu_custom_call" | custom-call | bytes 1572864 | tf_op jit(solution)/shard_map/pack/pallas_call | solution.py:215
  33.6 3.7 %all-to-all-start = ((bf16[16,2,32,384]{3,2,1,0:T(8,128)(2,1)}), bf16[16,2,32,384]{3,2,1,0:T(8,128)(2,1)S(1)}, u32[]{:S(2)}, u32[]{:S(2)}) async-start(bf16[16,2,32,384]{3,2,1,0:T(8,128)(2,1)} %get-tuple-element.33), calls=%async_computation | async-start | bytes 1572864 | tf_op jit(solution)/shard_map/all_to_all | solution.py:225
  37.3 0.8 constant_dynamic-slice_fusion
  38.1 1.9 %collective-permute-start = (bf16[8,48,384]{2,1,0:T(8,128)(2,1)}, bf16[8,48,384]{2,1,0:T(8,128)(2,1)S(1)}, u32[]{:S(2)}, u32[]{:S(2)}) collective-permute-start(bf16[8,48,384]{2,1,0:T(8,128)(2,1)} %constant_dynamic-slice_fusion), channel_id=1, source_target_pairs={{0,128},{128,256},{256,384},{384,0},{1,129},{129,257},{257,385},{3... | collective-permute-start | bytes 884744 | tf_op jit(solution)/shard_map/ppermute | solution.py:229
  40.0 4.2 %collective-permute-start.1 = (bf16[8,48,384]{2,1,0:T(8,128)(2,1)}, bf16[8,48,384]{2,1,0:T(8,128)(2,1)S(1)}, u32[]{:S(2)}, u32[]{:S(2)}) collective-permute-start(bf16[8,48,384]{2,1,0:T(8,128)(2,1)} %constant_dynamic-slice_fusion), channel_id=1, source_target_pairs={{0,256},{128,384},{256,0},{384,128},{1,257},{129,385},{257,1},{385... | collective-permute-start | bytes 884744 | tf_op jit(solution)/shard_map/ppermute | solution.py:229
  44.2 3.1 %collective-permute-start.2 = (bf16[8,48,384]{2,1,0:T(8,128)(2,1)}, bf16[8,48,384]{2,1,0:T(8,128)(2,1)S(1)}, u32[]{:S(2)}, u32[]{:S(2)}) collective-permute-start(bf16[8,48,384]{2,1,0:T(8,128)(2,1)} %constant_dynamic-slice_fusion), channel_id=1, source_target_pairs={{0,384},{128,0},{256,128},{384,256},{1,385},{129,1},{257,129},{385... | collective-permute-start | bytes 884744 | tf_op jit(solution)/shard_map/ppermute | solution.py:229
  47.4 12.6 %all-to-all-done.got = bf16[16,2,32,384]{3,2,1,0:T(8,128)(2,1)S(1)} async-done(((bf16[16,2,32,384]{3,2,1,0:T(8,128)(2,1)}), bf16[16,2,32,384]{3,2,1,0:T(8,128)(2,1)S(1)}, u32[]{:S(2)}, u32[]{:S(2)}) %all-to-all-start) | async-done | bytes 786464 | tf_op jit(solution)/shard_map/all_to_all | solution.py:225
  60.0 2.7 %attend.1.attn = bf16[256,384]{1,0:T(8,128)(2,1)S(1)} custom-call(s32[16]{0:T(128)S(1)} %and_select_fusion.lookup, bf16[8,32,384]{2,1,0:T(8,128)(2,1)S(1)} %copy-done.4, bf16[8,32,384]{2,1,0:T(8,128)(2,1)S(1)} %get-tuple-element.31.keys, bf16[8,32,384]{2,1,0:T(8,128)(2,1)S(1)} %get-tuple-element.32.values, bf16[16,2,32,384]{3,2,1,0:T(8,128)(2,1)S(1)} %all-to-all-done.got), custom_call_target="tpu_custom_call" | custom-call | flops 2000000000 | bytes 8000000 | tf_op jit(solution)/shard_map/attend/pallas_call | solution.py:238
  62.8 1.3 %send.1 = bf16[8,192,384]{2,1,0:T(8,128)(2,1)S(1)} custom-call(s32[1]{0:T(128)} %bitcast.5.side, bf16[8,256,384]{2,1,0:T(8,128)(2,1)S(1)} %copy-done.3, bf16[256,384]{1,0:T(8,128)(2,1)S(1)} %attend.1.attn), custom_call_target="tpu_custom_call" | custom-call | flops 3000000000 | bytes 3000000 | tf_op jit(solution)/shard_map/send/pallas_call | solution.py:251
  64.1 1.9 %collective-permute-start.4 = (bf16[8,192,384]{2,1,0:T(8,128)(2,1)S(1)}, bf16[8,192,384]{2,1,0:T(8,128)(2,1)S(1)}, u32[]{:S(2)}, u32[]{:S(2)}) collective-permute-start(bf16[8,192,384]{2,1,0:T(8,128)(2,1)S(1)} %send.1), channel_id=1, source_target_pairs={{0,8},{8,0},{1,9},{9,1},{2,10},{10,2},{3,11},{11,3},{4,12},{12,4},... | collective-permute-start | bytes 3538952 | tf_op jit(solution)/shard_map/ppermute | solution.py:262
  66.1 2.4 %collective-permute-start.3 = (bf16[3,8,48,384]{3,2,1,0:T(8,128)(2,1)S(1)}, bf16[3,8,48,384]{3,2,1,0:T(8,128)(2,1)S(1)}, u32[]{:S(2)}, u32[]{:S(2)}) collective-permute-start(bf16[3,8,48,384]{3,2,1,0:T(8,128)(2,1)S(1)} %join.1.halves), channel_id=1, source_target_pairs={{0,8},{8,0},{1,9},{9,1},{2,10},{10,2},{3,11},{11,3},{4,12},{12,4},... | collective-permute-start | bytes 2654216 | tf_op jit(solution)/shard_map/ppermute | solution.py:282
  68.6 1.3 %keep.1.ours = bf16[8,192,384]{2,1,0:T(8,128)(2,1)S(1)} custom-call(s32[1]{0:T(128)} %bitcast.1.side, bf16[8,256,384]{2,1,0:T(8,128)(2,1)S(1)} %copy-done.3, bf16[256,384]{1,0:T(8,128)(2,1)S(1)} %attend.1.attn), custom_call_target="tpu_custom_call" | custom-call | flops 3000000000 | bytes 3000000 | tf_op jit(solution)/shard_map/keep/pallas_call | solution.py:251
  69.9 1.1 add.36
  71.2 0.9 copy-done.5
  72.1 0.9 copy-done.7
  73.0 0.9 copy-done.9
  73.9 0.9 copy-done.11
  74.9 7.1 %backward.1 = (bf16[8,32,384]{2,1,0:T(8,128)(2,1)}, bf16[16,2,32,384]{3,2,1,0:T(8,128)(2,1)S(1)}, f32[256,384]{1,0:T(8,128)S(1)}, f32[256,384]{1,0:T(8,128)S(1)}) custom-call(s32[16]{0:T(128)S(1)} %and_select_fusion.lookup, s32[2]{0:T(128)S(1)} %pad_add_fusion.place, bf16[8,32,384]{2,1,0:T(8,128)(2,1)S(1)} %copy-done.5, bf16[8,32,384]{2,1,0:T(8,128)(2,1)S(1)} %copy-done.7, ...), custom_call_target="tpu_custom_call" | custom-call | flops 6000000000 | bytes 9000000 | tf_op jit(solution)/shard_map/backward/pallas_call | solution.py:285
  82.0 34.3 %all_to_all.10.came = bf16[16,2,32,384]{3,2,1,0:T(8,128)(2,1)S(1)} all-to-all(bf16[16,2,32,384]{3,2,1,0:T(8,128)(2,1)S(1)} %get-tuple-element.41), channel_id=1, replica_groups=mesh['dp'=4,'y'=8,'core'=2,'head'=8] {'y','core'}, dimensions={0} | all-to-all | bytes 1572864 | tf_op jit(solution)/shard_map/all_to_all | solution.py:316
  116.3 1.5 %finish.1 = (bf16[8,32,384]{2,1,0:T(8,128)(2,1)}, bf16[8,32,384]{2,1,0:T(8,128)(2,1)}) custom-call(s32[16]{0:T(128)S(1)} %fusion.4.source, bf16[16,2,32,384]{3,2,1,0:T(8,128)(2,1)S(1)} %all_to_all.10.came, f32[256,384]{1,0:T(8,128)S(1)} %get-tuple-element.42.own_dk, f32[256,384]{1,0:T(8,128)S(1)} %get-tuple-element.43.own_dv), custom_call_target="tpu_custom_call" | custom-call | flops 1000000 | bytes 3000000 | tf_op jit(solution)/shard_map/finish/pallas_call | solution.py:318
  117.8 1.1 reduce-scatter.2.cloned.1.call-done
  118.9 1.6 %bitcast_convert_fusion = f32[192,384]{1,0:T(8,128)} fusion(bf16[1,192,384]{2,1,0:T(8,128)(2,1)} %reduce-scatter.2.cloned.1.call-done), kind=kLoop, calls=%fused_computation | loop fusion | flops 73728 | bytes 442368 | tf_op jit(solution)/shard_map/convert_element_type | solution.py:328
  (41 shorter events, 1.3 us)
Async XLA Ops:
  7.2 1.6 %copy-start = (bf16[192,384]{1,0:T(8,128)(2,1)S(1)}, bf16[192,384]{1,0:T(8,128)(2,1)}, u32[]{:S(2)}) copy-start(bf16[192,384]{1,0:T(8,128)(2,1)} %param.12) | copy-start | bytes 442372
  7.2 24.9 %copy-start.1 = (bf16[8,32,384]{2,1,0:T(8,128)(2,1)S(1)}, bf16[8,32,384]{2,1,0:T(8,128)(2,1)}, u32[]{:S(2)}) copy-start(bf16[8,32,384]{2,1,0:T(8,128)(2,1)} %keys.1) | copy-start | bytes 589828
  7.2 24.8 %copy-start.2 = (bf16[8,32,384]{2,1,0:T(8,128)(2,1)S(1)}, bf16[8,32,384]{2,1,0:T(8,128)(2,1)}, u32[]{:S(2)}) copy-start(bf16[8,32,384]{2,1,0:T(8,128)(2,1)} %values.1) | copy-start | bytes 589828
  7.2 52.8 %all-gather.3.cloned.1.call-start = ((), (), s32[]{:S(2)}) async-start(), calls=%async_computation.3 | async-start | bytes 1769472 | tf_op jit(solution)/shard_map/all_gather | solution.py:206
  33.6 29.2 %copy-start.6 = (bf16[8,32,384]{2,1,0:T(8,128)(2,1)}, bf16[8,32,384]{2,1,0:T(8,128)(2,1)S(1)}, u32[]{:S(2)}) copy-start(bf16[8,32,384]{2,1,0:T(8,128)(2,1)S(1)} %get-tuple-element.31.keys) | copy-start | bytes 589828
  33.6 29.2 %copy-start.8 = (bf16[8,32,384]{2,1,0:T(8,128)(2,1)}, bf16[8,32,384]{2,1,0:T(8,128)(2,1)S(1)}, u32[]{:S(2)}) copy-start(bf16[8,32,384]{2,1,0:T(8,128)(2,1)S(1)} %get-tuple-element.32.values) | copy-start | bytes 589828
  33.6 13.7 %copy-start.12 = (s32[2,8]{1,0:T(2,128)S(1)}, s32[2,8]{1,0:T(2,128)}, u32[]{:S(2)}) copy-start(s32[2,8]{1,0:T(2,128)} %param.13) | copy-start | bytes 196
  33.6 26.4 %copy-start.4 = (bf16[8,32,384]{2,1,0:T(8,128)(2,1)S(1)}, bf16[8,32,384]{2,1,0:T(8,128)(2,1)}, u32[]{:S(2)}) copy-start(bf16[8,32,384]{2,1,0:T(8,128)(2,1)} %queries.3) | copy-start | bytes 589828
  33.6 26.4 %all-to-all-start = ((bf16[16,2,32,384]{3,2,1,0:T(8,128)(2,1)}), bf16[16,2,32,384]{3,2,1,0:T(8,128)(2,1)S(1)}, u32[]{:S(2)}, u32[]{:S(2)}) async-start(bf16[16,2,32,384]{3,2,1,0:T(8,128)(2,1)} %get-tuple-element.33), calls=%async_computation | async-start | bytes 1572864 | tf_op jit(solution)/shard_map/all_to_all | solution.py:225
  37.3 81.6 %reduce-scatter.2.cloned.1.call-start = ((), (), s32[]{:S(2)}) async-start(), calls=%async_computation.4 | async-start | bytes 1327104 | tf_op jit(solution)/shard_map/reduce_scatter | solution.py:283
  38.1 24.7 %collective-permute-start = (bf16[8,48,384]{2,1,0:T(8,128)(2,1)}, bf16[8,48,384]{2,1,0:T(8,128)(2,1)S(1)}, u32[]{:S(2)}, u32[]{:S(2)}) collective-permute-start(bf16[8,48,384]{2,1,0:T(8,128)(2,1)} %constant_dynamic-slice_fusion), channel_id=1, source_target_pairs={{0,128},{128,256},{256,384},{384,0},{1,129},{129,257},{257,385},{3... | collective-permute-start | bytes 884744 | tf_op jit(solution)/shard_map/ppermute | solution.py:229
  40.0 22.8 %collective-permute-start.1 = (bf16[8,48,384]{2,1,0:T(8,128)(2,1)}, bf16[8,48,384]{2,1,0:T(8,128)(2,1)S(1)}, u32[]{:S(2)}, u32[]{:S(2)}) collective-permute-start(bf16[8,48,384]{2,1,0:T(8,128)(2,1)} %constant_dynamic-slice_fusion), channel_id=1, source_target_pairs={{0,256},{128,384},{256,0},{384,128},{1,257},{129,385},{257,1},{385... | collective-permute-start | bytes 884744 | tf_op jit(solution)/shard_map/ppermute | solution.py:229
  44.2 18.6 %collective-permute-start.2 = (bf16[8,48,384]{2,1,0:T(8,128)(2,1)}, bf16[8,48,384]{2,1,0:T(8,128)(2,1)S(1)}, u32[]{:S(2)}, u32[]{:S(2)}) collective-permute-start(bf16[8,48,384]{2,1,0:T(8,128)(2,1)} %constant_dynamic-slice_fusion), channel_id=1, source_target_pairs={{0,384},{128,0},{256,128},{384,256},{1,385},{129,1},{257,129},{385... | collective-permute-start | bytes 884744 | tf_op jit(solution)/shard_map/ppermute | solution.py:229
  60.0 2.8 %copy-start.3 = (bf16[8,256,384]{2,1,0:T(8,128)(2,1)S(1)}, bf16[8,256,384]{2,1,0:T(8,128)(2,1)}, u32[]{:S(2)}) copy-start(bf16[8,256,384]{2,1,0:T(8,128)(2,1)} %all-gather.3.cloned.1.call-done.grad_far.grad) | copy-start | bytes 4718596
  62.8 5.8 %copy-start.10 = (bf16[256,384]{1,0:T(8,128)(2,1)}, bf16[256,384]{1,0:T(8,128)(2,1)S(1)}, u32[]{:S(2)}) copy-start(bf16[256,384]{1,0:T(8,128)(2,1)S(1)} %attend.1.attn) | copy-start | bytes 589828
  64.1 5.8 %collective-permute-start.4 = (bf16[8,192,384]{2,1,0:T(8,128)(2,1)S(1)}, bf16[8,192,384]{2,1,0:T(8,128)(2,1)S(1)}, u32[]{:S(2)}, u32[]{:S(2)}) collective-permute-start(bf16[8,192,384]{2,1,0:T(8,128)(2,1)S(1)} %send.1), channel_id=1, source_target_pairs={{0,8},{8,0},{1,9},{9,1},{2,10},{10,2},{3,11},{11,3},{4,12},{12,4},... | collective-permute-start | bytes 3538952 | tf_op jit(solution)/shard_map/ppermute | solution.py:262
  66.1 5.0 %collective-permute-start.3 = (bf16[3,8,48,384]{3,2,1,0:T(8,128)(2,1)S(1)}, bf16[3,8,48,384]{3,2,1,0:T(8,128)(2,1)S(1)}, u32[]{:S(2)}, u32[]{:S(2)}) collective-permute-start(bf16[3,8,48,384]{3,2,1,0:T(8,128)(2,1)S(1)} %join.1.halves), channel_id=1, source_target_pairs={{0,8},{8,0},{1,9},{9,1},{2,10},{10,2},{3,11},{11,3},{4,12},{12,4},... | collective-permute-start | bytes 2654216 | tf_op jit(solution)/shard_map/ppermute | solution.py:282
  71.2 0.9 copy-start.5
  72.1 0.9 copy-start.7
  73.0 0.9 copy-start.9
  73.9 0.9 copy-start.11
Sparse Core Ops, SparseCore 0:
  10.1 45.0 all-gather.2
  71.2 47.6 reduce-scatter.1
